TPU v7x, 128 devices: a whole 4x4x4 slice. The times are simulated.
128 devices in a mesh: sec: 32 (over y, x_lo, z), strip: 4 (over x_hi, core).
Axes of the slice: x: 4 (x_hi: 2, x_lo: 2; x = x_hi * 2 + x_lo), y: 4, z: 4, core: 2. Of those that a mesh axis runs over, the one named last changes fastest.
Arguments:
- images: bfloat16 [32, 2048, 2048], P('sec', 'strip'), may hold values from -8 to 8
- offsets: int32 [25, 2], replicated, may hold values from -3 to 3, as said below
- springs: int32 [2, 32, 512, 512], P(None, 'sec', 'strip'), may hold values from 1 to 8
- validity: int32 [32, 512, 512], P('sec', 'strip'), may hold values 0 or 1
Outputs:
- relaxed: float32 [2, 32, 512, 512], P(None, 'sec', 'strip')
Inputs may be any that keep to these rules, and one draw needn't show every extreme that they name: `offsets`: 25 distinct displacements; among them (0, 0), (-3, -3) and (3, 3).
All inputs are finite; a program needn't handle non-finite values. No bound on the sum of `validity` on one device may be relied on, other than what follows from the above.
Results may differ from a plain program's by a relative error of at most 0.0015.
Values may be sent and summed in bfloat16 or wider, within the bound.
A program may use at most 128 MiB of HBM per device.

v0:
```python
import jax
import jax.numpy as jnp
from jax import lax
from jax.sharding import PartitionSpec as P

RAD = 3
ITERS = 8


sharpness = 0.5
relax_rate = 0.8


def shifted_2(shard, axis, by):
    size = lax.axis_size(axis)
    pairs = [(i, i + by) for i in range(size) if 0 <= i + by < size]
    return lax.ppermute(shard, axis, pairs)


def extended(cells, sides, width):
    for axis, dim in sides:
        count = lax.axis_size(axis)
        ends = count - 1
        head = lax.slice_in_dim(cells, 0, width, axis=dim)
        tail = lax.slice_in_dim(cells, cells.shape[dim] - width, cells.shape[dim], axis=dim)
        cells = jnp.concatenate(
            [
                lax.ppermute(tail, axis, [(i, (i + 1) % count) for i in range(ends)]),
                cells,
                lax.ppermute(head, axis, [((i + 1) % count, i) for i in range(ends)]),
            ],
            axis=dim,
        )
    return cells


def section_flow(current, padded, offsets):
    row_count, col_count = current.shape
    current_f = current.astype(jnp.float32)
    column_ids = jnp.arange(col_count, dtype=jnp.int32)[:, None] // 4
    node_ids = jnp.arange(col_count // 4, dtype=jnp.int32)[None, :]
    pooling = (column_ids == node_ids).astype(jnp.float32)

    def one_offset(offset):
        shifted = lax.dynamic_slice(
            padded, (RAD + offset[0], RAD + offset[1]), (row_count, col_count)
        ).astype(jnp.float32)
        product = current_f * shifted
        row_pooled = product.reshape(row_count // 4, 4, col_count).sum(axis=1)
        return sharpness * jnp.dot(
            row_pooled, pooling, precision=lax.Precision.HIGHEST, preferred_element_type=jnp.float32
        )

    scores = lax.map(one_offset, offsets)
    highest = jnp.max(scores, axis=0)
    soft_weights = jnp.exp(scores - highest)
    weight_sum = jnp.sum(soft_weights, axis=0)
    shifts = offsets.astype(jnp.float32)
    flow_row = jnp.sum(soft_weights * shifts[:, 0, None, None], axis=0) / weight_sum
    flow_col = jnp.sum(soft_weights * shifts[:, 1, None, None], axis=0) / weight_sum
    return jnp.stack([flow_row, flow_col])


def advance(
    positions,
    from_below,
    from_above,
    from_right,
    from_left,
    row_weight,
    weight_up,
    col_weight,
    weight_left,
    pull_term,
    pull_prior,
    diagonal,
):
    force = row_weight * (from_below - positions) + weight_up * (from_above - positions)
    force = force + col_weight * (from_right - positions) + weight_left * (from_left - positions)
    force = force + pull_term - pull_prior
    return positions + relax_rate * force / (1.0 + diagonal)


def shards(images, offsets, springs, validity):
    successor = shifted_2(images, "sec", -1)
    rimmed = extended(successor, (("strip", 1),), RAD)
    padded = jnp.pad(rimmed[0], ((0, 0), (RAD, RAD)))
    flow_field = section_flow(images[0], padded, offsets)
    keep_mask = (lax.axis_index("sec") < lax.axis_size("sec") - 1).astype(jnp.float32)
    flow_field = flow_field * keep_mask
    node_rows, node_cols = (flow_field.shape[1], flow_field.shape[2])
    global_rows = lax.axis_index("strip") * node_rows + jnp.arange(node_rows, dtype=jnp.int32)
    row_keep = (global_rows < node_rows * lax.axis_size("strip") - 1).astype(jnp.float32)
    col_keep = (jnp.arange(node_cols) < node_cols - 1).astype(jnp.float32)
    row_weight = 0.25 * springs[0, 0].astype(jnp.float32) * row_keep[:, None]
    col_weight = 0.25 * springs[1, 0].astype(jnp.float32) * col_keep[None, :]
    match_weight = validity[0].astype(jnp.float32) * keep_mask
    row_above = shifted_2(row_weight[-1:], "strip", 1)
    weight_up = jnp.concatenate([row_above, row_weight[:-1]], axis=0)
    weight_left = jnp.pad(col_weight, ((0, 0), (1, 0)))[:, :-1]
    match_prior = shifted_2(match_weight.astype(jnp.bfloat16), "sec", 1).astype(match_weight.dtype)
    diagonal = row_weight + weight_up + col_weight + weight_left + match_weight + match_prior
    positions = jnp.zeros_like(flow_field)
    for iteration in range(ITERS):
        haloed = extended(positions.astype(jnp.bfloat16), (("strip", 1),), 1).astype(
            positions.dtype
        )
        sideways = jnp.pad(positions, ((0, 0), (0, 0), (1, 1)))
        following = shifted_2(positions.astype(jnp.bfloat16), "sec", -1).astype(positions.dtype)
        pull_term = match_weight * (following - positions - flow_field)
        pull_prior = shifted_2(pull_term, "sec", 1)
        positions = advance(
            positions,
            haloed[:, 2:],
            haloed[:, :-2],
            sideways[:, :, 2:],
            sideways[:, :, :-2],
            row_weight,
            weight_up,
            col_weight,
            weight_left,
            pull_term,
            pull_prior,
            diagonal,
        )
    return positions[:, None]


def solution(mesh):
    in_specs = (
        P("sec", "strip", None),
        P(),
        P(None, "sec", "strip", None),
        P("sec", "strip", None),
    )
    out_specs = P(None, "sec", "strip", None)
    return jax.shard_map(shards, mesh=mesh, in_specs=in_specs, out_specs=out_specs, check_vma=False)
```

profile of v0, /device:TPU:0, one launch (start us, length us, event | category | flops | bytes accessed | tf_op | source)
XLA Modules:
  0.0 874.2 jit_solution(194452126850258885)
XLA Ops:
  12.5 38.1 %collective-permute-done.4 = bf16[1,512,2048]{2,1,0:T(8,128)(2,1)S(1)} collective-permute-done((bf16[1,512,2048]{2,1,0:T(8,128)(2,1)}, bf16[1,512,2048]{2,1,0:T(8,128)(2,1)S(1)}, u32[]{:S(2)}, u32[]{:S(2)}) %collective-permute-start.4) | collective-permute-done | bytes 2097184 | tf_op jit(solution)/shard_map/ppermute | solution.py:17
  60.7 611.0 %while.13 = (s32[]{:T(128)}, f32[25,128,512]{2,1,0:T(8,128)}, s32[25,2]{0,1:T(2,128)S(1)}, bf16[518,2054]{1,0:T(8,128)(2,1)S(1)}, f32[512,2048]{1,0:T(8,128)}, /...) while((s32[]{:T(128)}, f32[25,128,512]{2,1,0:T(8,128)}, ...), condition=%wide.region_2.3_spmd.clone, body=%wide.region_0.2_spmd.clone.sunk | while | flops 1615659008 | bytes 25436928 | solution.py:54
  74.6 5.8 reduce_sum.47
  147.9 5.8 reduce_sum.47
  172.3 5.8 reduce_sum.47
  196.8 5.8 reduce_sum.47
  221.2 5.8 reduce_sum.47
  270.1 5.8 reduce_sum.47
  294.6 5.8 reduce_sum.47
  319.0 5.8 reduce_sum.47
  343.5 5.8 reduce_sum.47
  441.2 5.8 reduce_sum.47
  465.6 5.8 reduce_sum.47
  490.0 5.8 reduce_sum.47
  696.1 7.6 collective-permute-done.11
  721.3 10.1 %collective-permute-done.15 = bf16[2,128,512]{2,1,0:T(8,128)(2,1)S(1)} collective-permute-done((bf16[2,128,512]{2,1,0:T(8,128)(2,1)S(1)}, bf16[2,128,512]{2,1,0:T(8,128)(2,1)S(1)}, u32[]{:S(2)}, u32[]{:S(2)}) %collective-permute-start.15) | collective-permute-done | bytes 262176 | tf_op jit(solution)/shard_map/ppermute | solution.py:17
  731.7 7.0 collective-permute-start.16
  743.7 6.5 collective-permute-done.16
  752.1 9.0 %collective-permute-done.19 = bf16[2,128,512]{2,1,0:T(8,128)(2,1)S(1)} collective-permute-done((bf16[2,128,512]{2,1,0:T(8,128)(2,1)S(1)}, bf16[2,128,512]{2,1,0:T(8,128)(2,1)S(1)}, u32[]{:S(2)}, u32[]{:S(2)}) %collective-permute-start.19) | collective-permute-done | bytes 262176 | tf_op jit(solution)/shard_map/ppermute | solution.py:17
  778.7 8.4 collective-permute-done.23
  787.3 6.1 collective-permute-start.24
  805.4 7.4 collective-permute-done.27
  829.7 8.0 collective-permute-done.31
  853.1 7.4 collective-permute-done.35
  (257 shorter events, 621.9 us)
Async XLA Ops:
  0.0 50.6 %collective-permute-start.4 = (bf16[1,512,2048]{2,1,0:T(8,128)(2,1)}, bf16[1,512,2048]{2,1,0:T(8,128)(2,1)S(1)}, u32[]{:S(2)}, u32[]{:S(2)}) collective-permute-start(bf16[1,512,2048]{2,1,0:T(8,128)(2,1)} %param.6), channel_id=1, source_target_pairs={{4,0},{8,4},{12,8},{16,12},{20,16},{24,20},{28,24},{32,28},{36,32}... | collective-permute-start | bytes 6291464 | tf_op jit(solution)/shard_map/ppermute | solution.py:17
  1.3 688.9 %collective-permute-start = (bf16[2,1,512]{2,1,0:T(2,128)(2,1)S(1)}, bf16[2,1,512]{2,1,0:T(2,128)(2,1)S(1)}, u32[]{:S(2)}, u32[]{:S(2)}) collective-permute-start(bf16[2,1,512]{2,1,0:T(2,128)(2,1)S(1)} %slice.186), channel_id=1, source_target_pairs={{0,1},{1,2},{2,3},{4,5},{5,6},{6,7},{8,9},{9,10},{10,11},{12,13},{... | collective-permute-start | bytes 6152 | tf_op jit(solution)/shard_map/ppermute | solution.py:28
  2.6 687.7 %collective-permute-start.1 = (bf16[2,1,512]{2,1,0:T(2,128)(2,1)S(1)}, bf16[2,1,512]{2,1,0:T(2,128)(2,1)S(1)}, u32[]{:S(2)}, u32[]{:S(2)}) collective-permute-start(bf16[2,1,512]{2,1,0:T(2,128)(2,1)S(1)} %slice.186), channel_id=1, source_target_pairs={{1,0},{2,1},{3,2},{5,4},{6,5},{7,6},{9,8},{10,9},{11,10},{13,12},{... | collective-permute-start | bytes 6152 | tf_op jit(solution)/shard_map/ppermute | solution.py:30
  4.6 674.7 %collective-permute-start.3 = (bf16[2,128,512]{2,1,0:T(8,128)(2,1)}, bf16[2,128,512]{2,1,0:T(8,128)(2,1)}, u32[]{:S(2)}, u32[]{:S(2)}) collective-permute-start(bf16[2,128,512]{2,1,0:T(8,128)(2,1)} %broadcast_in_dim.13), channel_id=1, source_target_pairs={{4,0},{8,4},{12,8},{16,12},{20,16},{24,20},{28,24},{32,28},{36,32}... | collective-permute-start | bytes 786440 | tf_op jit(solution)/shard_map/ppermute | solution.py:17
  51.9 6.4 collective-permute-start.6
  53.2 638.1 %collective-permute-start.8 = (bf16[128,512]{1,0:T(8,128)(2,1)}, bf16[128,512]{1,0:T(8,128)(2,1)S(1)}, u32[]{:S(2)}, u32[]{:S(2)}) collective-permute-start(bf16[128,512]{1,0:T(8,128)(2,1)} %get-tuple-element.130), channel_id=1, source_target_pairs={{0,4},{4,8},{8,12},{12,16},{16,20},{20,24},{24,28},{28,32},{32,36}... | collective-permute-start | bytes 393224 | tf_op jit(solution)/shard_map/ppermute | solution.py:17
  680.4 13.0 %collective-permute-start.7 = (f32[2,128,512]{2,1,0:T(8,128)S(1)}, f32[2,128,512]{2,1,0:T(8,128)S(1)}, u32[]{:S(2)}, u32[]{:S(2)}) collective-permute-start(f32[2,128,512]{2,1,0:T(8,128)S(1)} %subtract_multiply_fusion.7), channel_id=1, source_target_pairs={{0,4},{4,8},{8,12},{12,16},{16,20},{20,24},{24,28},{28,32},{32,36}... | collective-permute-start | bytes 1572872 | tf_op jit(solution)/shard_map/ppermute | solution.py:17
  684.3 7.0 collective-permute-start.2
  694.8 8.9 %collective-permute-start.11 = (bf16[2,128,512]{2,1,0:T(8,128)(2,1)S(1)}, bf16[2,128,512]{2,1,0:T(8,128)(2,1)S(1)}, u32[]{:S(2)}, u32[]{:S(2)}) collective-permute-start(bf16[2,128,512]{2,1,0:T(8,128)(2,1)S(1)} %get-tuple-element.126), channel_id=1, source_target_pairs={{4,0},{8,4},{12,8},{16,12},{20,16},{24,20},{28,24},{32,28},{36,32}... | collective-permute-start | bytes 786440 | tf_op jit(solution)/shard_map/ppermute | solution.py:17
  703.9 15.5 %collective-permute-start.12 = (f32[2,128,512]{2,1,0:T(8,128)S(1)}, f32[2,128,512]{2,1,0:T(8,128)S(1)}, u32[]{:S(2)}, u32[]{:S(2)}) collective-permute-start(f32[2,128,512]{2,1,0:T(8,128)S(1)} %subtract_multiply_fusion.6), channel_id=1, source_target_pairs={{0,4},{4,8},{8,12},{12,16},{16,20},{20,24},{24,28},{28,32},{32,36}... | collective-permute-start | bytes 1572872 | tf_op jit(solution)/shard_map/ppermute | solution.py:17
  708.8 6.1 collective-permute-start.10
  710.1 5.6 collective-permute-start.9
  720.0 11.4 %collective-permute-start.15 = (bf16[2,128,512]{2,1,0:T(8,128)(2,1)S(1)}, bf16[2,128,512]{2,1,0:T(8,128)(2,1)S(1)}, u32[]{:S(2)}, u32[]{:S(2)}) collective-permute-start(bf16[2,128,512]{2,1,0:T(8,128)(2,1)S(1)} %get-tuple-element.124), channel_id=1, source_target_pairs={{4,0},{8,4},{12,8},{16,12},{20,16},{24,20},{28,24},{32,28},{36,32}... | collective-permute-start | bytes 786440 | tf_op jit(solution)/shard_map/ppermute | solution.py:17
  731.7 18.5 %collective-permute-start.16 = (f32[2,128,512]{2,1,0:T(8,128)S(1)}, f32[2,128,512]{2,1,0:T(8,128)S(1)}, u32[]{:S(2)}, u32[]{:S(2)}) collective-permute-start(f32[2,128,512]{2,1,0:T(8,128)S(1)} %subtract_multiply_fusion.5), channel_id=1, source_target_pairs={{0,4},{4,8},{8,12},{12,16},{16,20},{20,24},{24,28},{28,32},{32,36}... | collective-permute-start | bytes 1572872 | tf_op jit(solution)/shard_map/ppermute | solution.py:17
  750.8 10.3 %collective-permute-start.19 = (bf16[2,128,512]{2,1,0:T(8,128)(2,1)S(1)}, bf16[2,128,512]{2,1,0:T(8,128)(2,1)S(1)}, u32[]{:S(2)}, u32[]{:S(2)}) collective-permute-start(bf16[2,128,512]{2,1,0:T(8,128)(2,1)S(1)} %get-tuple-element.122), channel_id=1, source_target_pairs={{4,0},{8,4},{12,8},{16,12},{20,16},{24,20},{28,24},{32,28},{36,32}... | collective-permute-start | bytes 786440 | tf_op jit(solution)/shard_map/ppermute | solution.py:17
  761.3 15.5 %collective-permute-start.20 = (f32[2,128,512]{2,1,0:T(8,128)S(1)}, f32[2,128,512]{2,1,0:T(8,128)S(1)}, u32[]{:S(2)}, u32[]{:S(2)}) collective-permute-start(f32[2,128,512]{2,1,0:T(8,128)S(1)} %subtract_multiply_fusion.4), channel_id=1, source_target_pairs={{0,4},{4,8},{8,12},{12,16},{16,20},{20,24},{24,28},{28,32},{32,36}... | collective-permute-start | bytes 1572872 | tf_op jit(solution)/shard_map/ppermute | solution.py:17
  777.4 9.7 %collective-permute-start.23 = (bf16[2,128,512]{2,1,0:T(8,128)(2,1)S(1)}, bf16[2,128,512]{2,1,0:T(8,128)(2,1)S(1)}, u32[]{:S(2)}, u32[]{:S(2)}) collective-permute-start(bf16[2,128,512]{2,1,0:T(8,128)(2,1)S(1)} %get-tuple-element.120), channel_id=1, source_target_pairs={{4,0},{8,4},{12,8},{16,12},{20,16},{24,20},{28,24},{32,28},{36,32}... | collective-permute-start | bytes 786440 | tf_op jit(solution)/shard_map/ppermute | solution.py:17
  787.3 16.2 %collective-permute-start.24 = (f32[2,128,512]{2,1,0:T(8,128)S(1)}, f32[2,128,512]{2,1,0:T(8,128)S(1)}, u32[]{:S(2)}, u32[]{:S(2)}) collective-permute-start(f32[2,128,512]{2,1,0:T(8,128)S(1)} %subtract_multiply_fusion.3), channel_id=1, source_target_pairs={{0,4},{4,8},{8,12},{12,16},{16,20},{20,24},{24,28},{28,32},{32,36}... | collective-permute-start | bytes 1572872 | tf_op jit(solution)/shard_map/ppermute | solution.py:17
  804.1 8.7 collective-permute-start.27
  813.0 14.8 %collective-permute-start.28 = (f32[2,128,512]{2,1,0:T(8,128)S(1)}, f32[2,128,512]{2,1,0:T(8,128)S(1)}, u32[]{:S(2)}, u32[]{:S(2)}) collective-permute-start(f32[2,128,512]{2,1,0:T(8,128)S(1)} %subtract_multiply_fusion.2), channel_id=1, source_target_pairs={{0,4},{4,8},{8,12},{12,16},{16,20},{20,24},{24,28},{28,32},{32,36}... | collective-permute-start | bytes 1572872 | tf_op jit(solution)/shard_map/ppermute | solution.py:17
  828.4 9.3 %collective-permute-start.31 = (bf16[2,128,512]{2,1,0:T(8,128)(2,1)S(1)}, bf16[2,128,512]{2,1,0:T(8,128)(2,1)S(1)}, u32[]{:S(2)}, u32[]{:S(2)}) collective-permute-start(bf16[2,128,512]{2,1,0:T(8,128)(2,1)S(1)} %get-tuple-element.116), channel_id=1, source_target_pairs={{4,0},{8,4},{12,8},{16,12},{20,16},{24,20},{28,24},{32,28},{36,32}... | collective-permute-start | bytes 786440 | tf_op jit(solution)/shard_map/ppermute | solution.py:17
  837.8 13.4 %collective-permute-start.32 = (f32[2,128,512]{2,1,0:T(8,128)S(1)}, f32[2,128,512]{2,1,0:T(8,128)S(1)}, u32[]{:S(2)}, u32[]{:S(2)}) collective-permute-start(f32[2,128,512]{2,1,0:T(8,128)S(1)} %subtract_multiply_fusion.1), channel_id=1, source_target_pairs={{0,4},{4,8},{8,12},{12,16},{16,20},{20,24},{24,28},{28,32},{32,36}... | collective-permute-start | bytes 1572872 | tf_op jit(solution)/shard_map/ppermute | solution.py:17
  851.8 8.7 collective-permute-start.35
  860.8 12.1 %collective-permute-start.36 = (f32[2,128,512]{2,1,0:T(8,128)S(1)}, f32[2,128,512]{2,1,0:T(8,128)S(1)}, u32[]{:S(2)}, u32[]{:S(2)}) collective-permute-start(f32[2,128,512]{2,1,0:T(8,128)S(1)} %subtract_multiply_fusion), channel_id=1, source_target_pairs={{0,4},{4,8},{8,12},{12,16},{16,20},{20,24},{24,28},{28,32},{32,36}... | collective-permute-start | bytes 1572872 | tf_op jit(solution)/shard_map/ppermute | solution.py:17
  (15 other events, 53.5 us)
where the time goes:
time: 891 us; the launch traced here: 874 us
  other arithmetic  307 us (34%)
  local copies, waits for them, and re-layouts  148 us (17%)
  waiting for transfers between devices  145 us (16%)
  matrix products  118 us (13%)
  starting transfers between devices  89.6 us (10%)
  loops' own time  65.9 us (7%)
    reduce_sum x25, other arithmetic, one_offset(): row_pooled = product.reshape(row_count // 4, 4, col_count).sum(axis=1)  146 us
    mul x25, other arithmetic, one_offset(): product = current_f * shifted  135 us
    ppermute x19, waiting for transfers between devices, shifted_2(): return lax.ppermute(shard, axis, pairs)  132 us
    reshape x25, local copies, waits for them, and re-layouts, one_offset(): row_pooled = product.reshape(row_count // 4, 4, col_count).sum(axis=1)  129 us
    dot_general x25, matrix products, one_offset(): jnp.dot(row_pooled, pooling, precision=lax.Precision.HIGHEST, preferred_e...  118 us
    another operation x1, loops' own time, section_flow(): scores = lax.map(one_offset, offsets)  65.9 us
    ppermute x19, starting transfers between devices, shifted_2(): return lax.ppermute(shard, axis, pairs)  62.4 us
  transfers between devices with their start and end apart: 37, of which 24 were waited for; matrix products, arithmetic and copies ran while one was open for 65% of the time, Pallas kernels for 0%

commit v1 on v0

v1 whole, which is shorter than its diff:
```python
import jax
import jax.numpy as jnp
from jax import lax
from jax.experimental import pallas as pl
from jax.experimental.pallas import tpu as pltpu
from jax.sharding import PartitionSpec as P

RAD = 3
ITERS = 8
SHARPNESS = 0.5
RELAX_RATE = 0.8
NOFF = 25

BF = jnp.bfloat16
F32 = jnp.float32
MESH = pl.DeviceIdType.MESH
HIGH = lax.Precision.HIGHEST

GROUP = 8
PIX = 64
NODES = 16
SPAN = 40
ORDER = (0, 1, 3, 2)


def part_of(e, t):
    n = jnp.where(e < 4, e, 11 - e)
    return jnp.where(t % 2 == 0, n, 7 - n)


def member_of(c, t):
    n = jnp.where(t % 2 == 0, c, 7 - c)
    return jnp.where(n < 4, n, 11 - n)


def iota(shape, dim):
    return lax.broadcasted_iota(jnp.int32, shape, dim)


def kernel(
    off_ref, x_ref, sp_ref, va_ref, out_ref,
    xs, got, ws, wgot, wup_s, wup_r, cur, nxt, tmp, hs, hr, coef, mf, e0s, e0r, rel, zed, ys, yr, rs_, rr_, ret,
    img_ss, img_rs, fwd_ss, fwd_rs, st_ss, st_rs, ms_ss, ms_rs, hl_ss, hl_rs, wu_ss, wu_rs, e0_ss, e0_rs,
    it_ss, it_rs, rt_ss, rt_rs,
):
    sec = lax.axis_index("sec")
    t = lax.axis_index("strip")
    y, e = sec // 8, sec % 8
    c = part_of(e, t)
    g = t * 8 + c

    def row_device(h):
        h = (h + 32) % 32
        tt = h // 8
        return (8 * y + member_of(h % 8, tt), tt)

    peers = [(8 * y + (e + k) % 8, t) for k in range(1, 8)]
    ynext = ((sec + 8) % 32, t)
    yprev = ((sec + 24) % 32, t)
    below = row_device(g + 1)
    above = row_device(g - 1)
    barrier = pltpu.get_barrier_semaphore()
    everyone = peers + [ynext, yprev, below, above]
    for d in everyone:
        pl.semaphore_signal(barrier, inc=1, device_id=d, device_id_type=MESH)

    source = iota((512, 512), 0)
    target = iota((512, 512), 1)
    spread = (source == 4 * (target % 128) + target // 128).astype(F32).astype(BF)

    def arrange(i, _):
        rows = pl.ds(pl.multiple_of(i * 128, 128), 128)
        for q in range(4):
            block = x_ref[0, rows, 512 * q : 512 * q + 512]
            xs[rows, 512 * q : 512 * q + 512] = jnp.dot(block, spread, preferred_element_type=F32).astype(BF)
        return 0

    lax.fori_loop(0, 4, arrange, 0)

    row_ids = iota((128, 512), 0)
    col_ids = iota((128, 512), 1)
    last_strip = lax.axis_size("strip") - 1
    wr_own = jnp.where((row_ids == 127) & (t == last_strip), 0.0, 0.25 * sp_ref[0, 0].astype(F32))
    wc_own = jnp.where(col_ids == 511, 0.0, 0.25 * sp_ref[1, 0].astype(F32))
    m_own = jnp.where(sec == lax.axis_size("sec") - 1, 0.0, va_ref[0].astype(F32))
    ws[0] = wr_own.astype(BF)
    ws[1] = wc_own.astype(BF)
    ws[2] = m_own.astype(BF)

    a = iota((128, 128), 0)
    b = iota((128, 128), 1)
    turn_f = (b == (a % 8) * 16 + a // 8).astype(F32)
    turn = turn_f.astype(BF)
    back = (a == (b % 8) * 16 + b // 8).astype(F32)

    pl.semaphore_wait(barrier, len(everyone))

    sends = []

    def remote(src, dst, ss, rs, dev):
        copy = pltpu.make_async_remote_copy(
            src_ref=src, dst_ref=dst, send_sem=ss, recv_sem=rs, device_id=dev, device_id_type=MESH
        )
        copy.start()
        sends.append(copy)
        return copy

    def image_copy(blk, k):
        other = (e + k) % 8
        oc = part_of(other, t)
        src = xs.at[pl.ds(pl.multiple_of(64 * oc + 16 * blk, 16), 16)]
        return pltpu.make_async_remote_copy(
            src_ref=src, dst_ref=got.at[e, pl.ds(16 * blk, 16)], send_sem=img_ss.at[blk, k],
            recv_sem=img_rs.at[blk, e], device_id=peers[k - 1], device_id_type=MESH,
        )

    def image_from(blk, s):
        return pltpu.make_async_remote_copy(
            src_ref=xs.at[pl.ds(0, 16)], dst_ref=got.at[s, pl.ds(16 * blk, 16)], send_sem=img_ss.at[blk, 0],
            recv_sem=img_rs.at[blk, s], device_id=peers[0], device_id_type=MESH,
        )

    def static_copy(k):
        other = (e + k) % 8
        oc = part_of(other, t)
        return pltpu.make_async_remote_copy(
            src_ref=ws.at[:, pl.ds(pl.multiple_of(16 * oc, 16), 16)], dst_ref=wgot.at[:, e + 1],
            send_sem=st_ss.at[k], recv_sem=st_rs.at[k], device_id=peers[k - 1], device_id_type=MESH,
        )

    started = []
    for n, blk in enumerate(ORDER):
        for k in range(1, 8):
            copy = image_copy(blk, k)
            copy.start()
            started.append(copy)
        if n == 0:
            statics = [static_copy(k) for k in range(1, 8)]
            for copy in statics:
                copy.start()
    got[e] = xs[pl.ds(pl.multiple_of(64 * c, 64), 64)]
    wgot[:, e + 1] = ws[:, pl.ds(pl.multiple_of(16 * c, 16), 16)]

    def forward(blk):
        @pl.when(e != 0)
        def _():
            image_from(blk, 0).wait_recv()

        return remote(got.at[0, pl.ds(16 * blk, 16)], got.at[8, pl.ds(16 * blk, 16)],
                      fwd_ss.at[blk], fwd_rs.at[blk], yprev)

    def arrive(blk):
        for s in range(1, 8):
            @pl.when(e != s)
            def _():
                image_from(blk, s).wait_recv()

    lane = iota((8, 128), 1)

    def expand(row, src_row):
        base = (row + RAD) * SPAN
        right, left = {}, {}
        for q in range(4):
            for w in range(4):
                plane = tmp[pl.ds(src_row, 8), 512 * q + 128 * w : 512 * q + 128 * w + 128]
                nxt[base + 10 * q + w + 3] = plane
                if w > 0:
                    right[q, w] = pltpu.roll(plane, 1, 1)
                if w < 3:
                    left[q, w] = pltpu.roll(plane, 127, 1)
        for q in range(4):
            for w in range(1, 4):
                carry = right[q - 1, w] if q else jnp.zeros((8, 128), F32)
                nxt[base + 10 * q + w - 1] = jnp.where(lane == 0, carry, right[q, w])
            for w in range(3):
                carry = left[q + 1, w] if q < 3 else jnp.zeros((8, 128), F32)
                nxt[base + 10 * q + w + 7] = jnp.where(lane == 127, carry, left[q, w])

    def convert(blk):
        rows = slice(16 * blk, 16 * blk + 16)
        here = jnp.dot(turn, got[0:8, rows].reshape(128, 2048), preferred_element_type=F32)
        for r in range(16):
            for p in range(16):
                cur[(16 * blk + r) * 16 + p] = here[8 * r : 8 * r + 8, 128 * p : 128 * p + 128]
        tmp[...] = jnp.dot(turn, got[1:9, rows].reshape(128, 2048), preferred_element_type=F32)

        def one(r, _):
            expand(16 * blk + r, pl.multiple_of(r * 8, 8))
            return 0

        lax.fori_loop(0, 16, one, 0)

    def score(first, count):
        def one(i, _):
            q4 = i % 4
            row = first + i // 4
            mine = [[cur[((4 * row + q) * 4 + q4) * 4 + w] for w in range(4)] for q in range(4)]
            scores = []
            for k in range(NOFF):
                at = (4 * row + off_ref[k, 0] + RAD) * SPAN + 10 * q4 + off_ref[k, 1] + RAD
                parts = []
                for q in range(4):
                    p = [mine[q][w] * nxt[at + (q * SPAN + w)] for w in range(4)]
                    parts.append((p[0] + p[1]) + (p[2] + p[3]))
                scores.append((parts[0] + parts[1]) + (parts[2] + parts[3]))
            top = scores[0]
            for k in range(1, NOFF):
                top = jnp.maximum(top, scores[k])
            total = jnp.zeros((8, 128), F32)
            down = jnp.zeros((8, 128), F32)
            side = jnp.zeros((8, 128), F32)
            for k in range(NOFF):
                soft = jnp.exp(SHARPNESS * (scores[k] - top))
                total += soft
                down += soft * off_ref[k, 0].astype(F32)
                side += soft * off_ref[k, 1].astype(F32)
            rows = pl.ds(pl.multiple_of(row * 8, 8), 8)
            match = coef[7, rows, pl.ds(pl.multiple_of(q4 * 128, 128), 128)]
            scale = match / total
            mf[rows, pl.ds(pl.multiple_of(q4 * 128, 128), 128)] = down * scale
            mf[rows, pl.ds(pl.multiple_of(512 + q4 * 128, 128), 128)] = side * scale
            return 0

        lax.fori_loop(0, 4 * count, one, 0)

    forwards = {}
    forwards[0] = forward(0)
    arrive(0)
    for copy in statics:
        copy.wait_recv()
    match_copy = remote(wgot.at[2, 8], wgot.at[2, 0], ms_ss, ms_rs, ynext)
    wr = jnp.dot(turn, wgot[0, 1:9].reshape(128, 512), preferred_element_type=F32)
    wup_s[...] = jnp.concatenate([wr[120:128], wr[120:128]], axis=0).astype(BF)
    up_copy = remote(wup_s, wup_r, wu_ss, wu_rs, below)
    wc = jnp.dot(turn, wgot[1, 1:9].reshape(128, 512), preferred_element_type=F32)
    m = jnp.dot(turn, wgot[2, 1:9].reshape(128, 512), preferred_element_type=F32)
    coef[0] = wr
    coef[2] = wc
    coef[7] = m

    forwards[0].wait_recv()
    convert(0)
    hs[0] = tmp[0:32].astype(BF)
    halo_up = remote(hs.at[0], hr.at[1], hl_ss.at[0], hl_rs.at[0], above)
    forwards[1] = forward(1)
    arrive(1)
    match_copy.wait_recv()
    up_copy.wait_recv()
    wr = coef[0]
    wc = coef[2]
    m = coef[7]
    mp = jnp.dot(turn, wgot[2, 0:8].reshape(128, 512), preferred_element_type=F32)
    wu = jnp.concatenate([wup_r[...].astype(F32)[0:8], wr[0:120]], axis=0)
    wl = jnp.where(col_ids == 0, 0.0, pltpu.roll(wc, 1, 1))
    diagonal = wr + wu + wc + wl + m + mp
    step = RELAX_RATE / (1.0 + diagonal)
    coef[0] = step * wr
    coef[1] = step * wu
    coef[2] = step * wc
    coef[3] = step * wl
    coef[4] = step * m
    coef[5] = step * mp
    coef[6] = 1.0 - step * diagonal
    coef[8] = step

    forwards[1].wait_recv()
    convert(1)
    forwards[3] = forward(3)
    score(1, 6)
    arrive(3)
    forwards[3].wait_recv()
    convert(3)
    hs[1] = tmp[96:128].astype(BF)
    halo_down = remote(hs.at[1], hr.at[0], hl_ss.at[1], hl_rs.at[1], below)
    forwards[2] = forward(2)
    score(13, 2)
    arrive(2)
    forwards[2].wait_recv()
    convert(2)
    score(7, 6)
    halo_up.wait_recv()
    halo_down.wait_recv()
    tmp[0:32] = jnp.where(g == 0, 0.0, hr[0].astype(F32))
    tmp[32:64] = jnp.where(g == 31, 0.0, hr[1].astype(F32))

    def head(r, _):
        expand(r - 3, pl.multiple_of(r * 8 + 8, 8))
        return 0

    lax.fori_loop(0, 3, head, 0)

    def foot(r, _):
        expand(PIX + r, pl.multiple_of(r * 8 + 32, 8))
        return 0

    lax.fori_loop(0, 3, foot, 0)
    score(0, 1)
    score(15, 1)

    u = iota((32, 128), 0)
    v = iota((32, 128), 1)
    pick_f = (v == jnp.where(u < 16, u * 8 + 7, (u - 16) * 8)).astype(F32)
    pick = pick_f.astype(BF)
    u = iota((128, 32), 1)
    v = iota((128, 32), 0)
    put_f = (v == jnp.where(u < 16, u * 8, (u - 16) * 8 + 7)).astype(F32)
    put = put_f.astype(BF)
    e0s[...] = jnp.dot(pick_f[0:16], mf[...], precision=HIGH, preferred_element_type=F32)
    e0 = remote(e0s, e0r, e0_ss, e0_rs, ynext)
    e0.wait_recv()
    zed[...] = jnp.dot(put_f[:, 0:16], e0r[...], precision=HIGH, preferred_element_type=F32)
    sub = iota((8, 512), 0)

    def begin(i, _):
        rows = pl.ds(pl.multiple_of(i * 8, 8), 8)
        for h in range(2):
            cols = slice(512 * h, 512 * h + 512)
            own = mf[rows, cols]
            before = jnp.where(sub == 0, zed[rows, cols], pltpu.roll(own, 1, 0))
            pushed = coef[8, rows] * (before - own)
            mf[rows, cols] = pushed
            rel[0, pl.ds(pl.multiple_of(i * 8 + 8, 8), 8), cols] = pushed
        return 0

    lax.fori_loop(0, NODES, begin, 0)

    def relax(n, _):
        old = n % 2
        new = 1 - old
        body = rel[old, 8:136]
        ys[n] = jnp.dot(pick, body.astype(BF), preferred_element_type=F32).astype(BF)
        rs_[n, 0] = jnp.concatenate([body[0:8, 0:512], body[0:8, 512:1024]], axis=0).astype(BF)
        rs_[n, 1] = jnp.concatenate([body[120:128, 0:512], body[120:128, 512:1024]], axis=0).astype(BF)
        copies = []
        for j, (src, dst, dev) in enumerate((
            (ys.at[n, pl.ds(0, 16)], yr.at[n, pl.ds(0, 16)], ynext),
            (ys.at[n, pl.ds(16, 16)], yr.at[n, pl.ds(16, 16)], yprev),
            (rs_.at[n, 0], rr_.at[n, 0], above),
            (rs_.at[n, 1], rr_.at[n, 1], below),
        )):
            copy = pltpu.make_async_remote_copy(
                src_ref=src, dst_ref=dst, send_sem=it_ss.at[n, j], recv_sem=it_rs.at[n, j],
                device_id=dev, device_id_type=MESH,
            )
            copy.start()
            copies.append(copy)
        for copy in copies:
            copy.wait()
        zed[...] = jnp.dot(put, yr[n], preferred_element_type=F32)
        low = rr_[n, 0].astype(F32)
        high = rr_[n, 1].astype(F32)
        rel[old, 136:144, 0:512] = low[0:8]
        rel[old, 136:144, 512:1024] = low[8:16]
        rel[old, 0:8, 0:512] = high[0:8]
        rel[old, 0:8, 512:1024] = high[8:16]

        def one(i, _):
            rows = pl.ds(pl.multiple_of(i * 8, 8), 8)
            mid = pl.ds(pl.multiple_of(i * 8 + 8, 8), 8)
            far = pl.ds(pl.multiple_of(i * 8 + 16, 8), 8)
            cs = [coef[k, rows] for k in range(7)]
            for h in range(2):
                cols = slice(512 * h, 512 * h + 512)
                own = rel[old, mid, cols]
                edge = zed[rows, cols]
                acc = mf[rows, cols] + cs[6] * own
                acc += cs[0] * rel[old, far, cols] + cs[1] * rel[old, rows, cols]
                acc += cs[2] * pltpu.roll(own, 511, 1) + cs[3] * pltpu.roll(own, 1, 1)
                acc += cs[4] * jnp.where(sub == 7, edge, pltpu.roll(own, 7, 0))
                acc += cs[5] * jnp.where(sub == 0, edge, pltpu.roll(own, 1, 0))
                rel[new, mid, cols] = acc
            return 0

        lax.fori_loop(0, NODES, one, 0)
        return 0

    lax.fori_loop(0, ITERS - 1, relax, 0)

    final = jnp.dot(back, rel[(ITERS - 1) % 2, 8:136], precision=HIGH, preferred_element_type=F32)
    ret[0] = final[:, 0:512]
    ret[1] = final[:, 512:1024]
    place = pl.ds(pl.multiple_of(16 * c, 16), 16)
    returns = []
    for k in range(1, 8):
        other = (e + k) % 8
        copy = pltpu.make_async_remote_copy(
            src_ref=ret.at[:, pl.ds(pl.multiple_of(16 * other, 16), 16)], dst_ref=out_ref.at[:, 0, place],
            send_sem=rt_ss.at[k], recv_sem=rt_rs.at[k], device_id=peers[k - 1], device_id_type=MESH,
        )
        copy.start()
        returns.append(copy)
    out_ref[:, 0, place] = ret[:, pl.ds(pl.multiple_of(16 * e, 16), 16)]
    for k in range(1, 8):
        oc = part_of((e + 8 - k) % 8, t)
        pltpu.make_async_remote_copy(
            src_ref=ret.at[:, pl.ds(0, 16)], dst_ref=out_ref.at[:, 0, pl.ds(pl.multiple_of(16 * oc, 16), 16)],
            send_sem=rt_ss.at[k], recv_sem=rt_rs.at[k], device_id=peers[k - 1], device_id_type=MESH,
        ).wait_recv()
    for copy in returns + started + statics + sends:
        copy.wait_send()


def shards(images, offsets, springs, validity):
    dma = pltpu.SemaphoreType.DMA
    vm = pltpu.VMEM
    whole = pl.BlockSpec(memory_space=pltpu.VMEM)
    return pl.pallas_call(
        kernel,
        out_shape=jax.ShapeDtypeStruct((2, 1, 128, 512), F32),
        in_specs=[pl.BlockSpec(memory_space=pltpu.SMEM), whole, whole, whole],
        out_specs=whole,
        scratch_shapes=[
            vm((512, 2048), BF),
            vm((9, PIX, 2048), BF),
            vm((3, 128, 512), BF),
            vm((3, 9, NODES, 512), BF),
            vm((16, 512), BF),
            vm((16, 512), BF),
            vm((PIX * 16, 8, 128), F32),
            vm(((PIX + 2 * RAD) * SPAN, 8, 128), F32),
            vm((128, 2048), F32),
            vm((2, 32, 2048), BF),
            vm((2, 32, 2048), BF),
            vm((9, 128, 512), F32),
            vm((128, 1024), F32),
            vm((16, 1024), F32),
            vm((16, 1024), F32),
            vm((2, 144, 1024), F32),
            vm((128, 1024), F32),
            vm((ITERS - 1, 32, 1024), BF),
            vm((ITERS - 1, 32, 1024), BF),
            vm((ITERS - 1, 2, 16, 512), BF),
            vm((ITERS - 1, 2, 16, 512), BF),
            vm((2, 128, 512), F32),
            dma((4, 8)), dma((4, 8)), dma((4,)), dma((4,)), dma((8,)), dma((8,)), dma, dma,
            dma((2,)), dma((2,)), dma, dma, dma, dma,
            dma((ITERS - 1, 4)), dma((ITERS - 1, 4)), dma((8,)), dma((8,)),
        ],
        compiler_params=pltpu.CompilerParams(
            collective_id=0, has_side_effects=True, vmem_limit_bytes=48 * 1024 * 1024
        ),
    )(offsets, images, springs, validity)


def solution(mesh):
    in_specs = (
        P("sec", "strip", None),
        P(),
        P(None, "sec", "strip", None),
        P("sec", "strip", None),
    )
    out_specs = P(None, "sec", "strip", None)
    return jax.shard_map(shards, mesh=mesh, in_specs=in_specs, out_specs=out_specs, check_vma=False)
```

time: 891 us -> 121 us (0.14); the launches traced: 874 us -> 121 us
  other arithmetic: 307 us -> 0 us
  waiting for transfers between devices: 145 us -> 0 us
  local copies, waits for them, and re-layouts: 148 us -> 5.15 us
  matrix products: 118 us -> 0 us
  Pallas kernels: 0 us -> 115 us
  starting transfers between devices: 89.6 us -> 0 us
  loops' own time: 65.9 us -> 0 us
    reduce_sum x26 -> x0, other arithmetic: 150 us -> none  [the longest x25 146 us: one_offset(): row_pooled = product.reshape(row_count // 4, 4, col_count).sum(axis=1)]
    ppermute x37 -> x0, waiting for transfers between devices: 145 us -> none  [the longest x19 132 us: shifted_2(): return lax.ppermute(shard, axis, pairs)]
    mul x36 -> x0, other arithmetic: 138 us -> none  [the longest x25 135 us: one_offset(): product = current_f * shifted]
    reshape x25 -> x0, local copies, waits for them, and re-layouts: 129 us -> none  [one_offset(): row_pooled = product.reshape(row_count // 4, 4, col_count).sum(axis=1)]
    dot_general x25 -> x0, matrix products: 118 us -> none  [one_offset(): jnp.dot(row_pooled, pooling, precision=lax.Precision.HIGHEST, preferred_e...]
    pallas_call x0 -> x1, Pallas kernels: none -> 115 us  [shards(): pl.pallas_call(kernel, out_shape=jax.ShapeDtypeStruct((2, 1, 128, 512), F...]
    ppermute x37 -> x0, starting transfers between devices: 89.6 us -> none  [the longest x19 62.4 us: shifted_2(): return lax.ppermute(shard, axis, pairs)]
    another operation x1 -> x0, loops' own time: 65.9 us -> none  [section_flow(): scores = lax.map(one_offset, offsets)]
  transfers between devices with their start and end apart: 37 -> 0, of which waited for: 24 -> 0; matrix products, arithmetic and copies ran while one was open for 65% -> 0% of each run, Pallas kernels for 0% -> 0%
where the time goes in v1:
time: 121 us
  Pallas kernels  115 us (95%)
  local copies, waits for them, and re-layouts  5.15 us (4%)
    pallas_call x1, Pallas kernels, shards(): pl.pallas_call(kernel, out_shape=jax.ShapeDtypeStruct((2, 1, 128, 512), F...  115 us
    unnamed x8, local copies, waits for them, and re-layouts  5.15 us

profile of v1, /device:TPU:0, one launch (start us, length us, event | category | flops | bytes accessed | tf_op | source)
XLA Modules:
  0.0 120.6 jit_solution(14217858241556667080)
XLA Ops:
  0.0 0.8 copy.5.off_ref
  0.8 0.0 copy-start
  0.8 1.6 %copy-done = bf16[1,512,2048]{2,1,0:T(8,128)(2,1)S(1)} copy-done((bf16[1,512,2048]{2,1,0:T(8,128)(2,1)S(1)}, bf16[1,512,2048]{2,1,0:T(8,128)(2,1)}, u32[]{:S(2)}) %copy-start) | copy-done | bytes 2097176
  2.4 0.0 copy-start.1
  2.4 1.0 copy-done.1
  3.4 0.0 copy-start.2
  3.4 0.9 copy-done.2
  4.4 115.5 %shard_map.46 = f32[2,1,128,512]{3,2,1,0:T(8,128)S(1)} custom-call(s32[25,2]{1,0:T(8,128)S(1)} %copy.5.off_ref, bf16[1,512,2048]{2,1,0:T(8,128)(2,1)S(1)} %copy-done, s32[2,1,128,512]{3,2,1,0:T(8,128)S(1)} %copy-done.1, s32[1,128,512]{2,1,0:T(8,128)S(1)} %copy-done.2), custom_call_target="tpu_custom_call" | custom-call | tf_op jit(solution)/shard_map/pallas_call | solution.py:407
  119.8 0.8 copy.7
Async XLA Ops:
  0.8 1.6 %copy-start = (bf16[1,512,2048]{2,1,0:T(8,128)(2,1)S(1)}, bf16[1,512,2048]{2,1,0:T(8,128)(2,1)}, u32[]{:S(2)}) copy-start(bf16[1,512,2048]{2,1,0:T(8,128)(2,1)} %x_ref.1) | copy-start | bytes 6291460
  2.4 1.0 copy-start.1
  3.4 0.9 copy-start.2

commit v2 on v1

--- a/solution.py
+++ b/solution.py
@@ -14,7 +14,6 @@
 BF = jnp.bfloat16
 F32 = jnp.float32
 MESH = pl.DeviceIdType.MESH
-HIGH = lax.Precision.HIGHEST
 
 GROUP = 8
 PIX = 64
@@ -33,15 +32,24 @@
     return jnp.where(n < 4, n, 11 - n)
 
 
+def load(ref, rows, first=0):
+    return jnp.concatenate([ref[first + q, rows, :] for q in range(4)], axis=1)
+
+
+def store(ref, rows, value, first=0):
+    for q in range(4):
+        ref[first + q, rows, :] = value[:, 128 * q : 128 * q + 128]
+
+
 def iota(shape, dim):
     return lax.broadcasted_iota(jnp.int32, shape, dim)
 
 
 def kernel(
-    off_ref, x_ref, sp_ref, va_ref, out_ref,
-    xs, got, ws, wgot, wup_s, wup_r, cur, nxt, tmp, hs, hr, coef, mf, e0s, e0r, rel, zed, ys, yr, rs_, rr_, ret,
+    off_hbm, x_hbm, sp_hbm, va_hbm, out_ref,
+    off_ref, x_ref, sp_ref, va_ref, xs, got, ws, wgot, wup_s, wup_r, cur, nxt, tmp, hs, hr, coef, cn7, cp0, mf, e0s, e0r, rel, ys, yr, rs_, rr_, ret,
     img_ss, img_rs, fwd_ss, fwd_rs, st_ss, st_rs, ms_ss, ms_rs, hl_ss, hl_rs, wu_ss, wu_rs, e0_ss, e0_rs,
-    it_ss, it_rs, rt_ss, rt_rs,
+    it_ss, it_rs, rt_ss, rt_rs, in_sem,
 ):
     sec = lax.axis_index("sec")
     t = lax.axis_index("strip")
@@ -64,34 +72,44 @@
     for d in everyone:
         pl.semaphore_signal(barrier, inc=1, device_id=d, device_id_type=MESH)
 
+    chunks = []
+    for i in range(4):
+        rows = pl.ds(128 * i, 128)
+        chunks.append(pltpu.make_async_copy(x_hbm.at[0, rows], x_ref.at[rows], in_sem.at[i]))
+    others = [
+        pltpu.make_async_copy(sp_hbm.at[:, 0], sp_ref, in_sem.at[4]),
+        pltpu.make_async_copy(va_hbm.at[0], va_ref, in_sem.at[5]),
+        pltpu.make_async_copy(off_hbm, off_ref, in_sem.at[6]),
+    ]
+    for copy in chunks + others:
+        copy.start()
+
     source = iota((512, 512), 0)
     target = iota((512, 512), 1)
     spread = (source == 4 * (target % 128) + target // 128).astype(F32).astype(BF)
 
-    def arrange(i, _):
-        rows = pl.ds(pl.multiple_of(i * 128, 128), 128)
+    for i in range(4):
+        chunks[i].wait()
+        rows = slice(128 * i, 128 * i + 128)
         for q in range(4):
-            block = x_ref[0, rows, 512 * q : 512 * q + 512]
-            xs[rows, 512 * q : 512 * q + 512] = jnp.dot(block, spread, preferred_element_type=F32).astype(BF)
-        return 0
-
-    lax.fori_loop(0, 4, arrange, 0)
+            cols = slice(512 * q, 512 * q + 512)
+            xs[rows, cols] = jnp.dot(x_ref[rows, cols], spread, preferred_element_type=F32).astype(BF)
+    for copy in others:
+        copy.wait()
 
     row_ids = iota((128, 512), 0)
     col_ids = iota((128, 512), 1)
     last_strip = lax.axis_size("strip") - 1
-    wr_own = jnp.where((row_ids == 127) & (t == last_strip), 0.0, 0.25 * sp_ref[0, 0].astype(F32))
-    wc_own = jnp.where(col_ids == 511, 0.0, 0.25 * sp_ref[1, 0].astype(F32))
-    m_own = jnp.where(sec == lax.axis_size("sec") - 1, 0.0, va_ref[0].astype(F32))
+    wr_own = jnp.where((row_ids == 127) & (t == last_strip), 0.0, 0.25 * sp_ref[0].astype(F32))
+    wc_own = jnp.where(col_ids == 511, 0.0, 0.25 * sp_ref[1].astype(F32))
+    m_own = jnp.where(sec == lax.axis_size("sec") - 1, 0.0, va_ref[...].astype(F32))
     ws[0] = wr_own.astype(BF)
     ws[1] = wc_own.astype(BF)
     ws[2] = m_own.astype(BF)
 
     a = iota((128, 128), 0)
     b = iota((128, 128), 1)
-    turn_f = (b == (a % 8) * 16 + a // 8).astype(F32)
-    turn = turn_f.astype(BF)
-    back = (a == (b % 8) * 16 + b // 8).astype(F32)
+    turn = (b == (a % 8) * 16 + a // 8).astype(F32).astype(BF)
 
     pl.semaphore_wait(barrier, len(everyone))
 
@@ -129,15 +147,14 @@
         )
 
     started = []
-    for n, blk in enumerate(ORDER):
+    for blk in ORDER:
         for k in range(1, 8):
             copy = image_copy(blk, k)
             copy.start()
             started.append(copy)
-        if n == 0:
-            statics = [static_copy(k) for k in range(1, 8)]
-            for copy in statics:
-                copy.start()
+    statics = [static_copy(k) for k in range(1, 8)]
+    for copy in statics:
+        copy.start()
     got[e] = xs[pl.ds(pl.multiple_of(64 * c, 64), 64)]
     wgot[:, e + 1] = ws[:, pl.ds(pl.multiple_of(16 * c, 16), 16)]
 
@@ -215,69 +232,32 @@
                 down += soft * off_ref[k, 0].astype(F32)
                 side += soft * off_ref[k, 1].astype(F32)
             rows = pl.ds(pl.multiple_of(row * 8, 8), 8)
-            match = coef[7, rows, pl.ds(pl.multiple_of(q4 * 128, 128), 128)]
-            scale = match / total
-            mf[rows, pl.ds(pl.multiple_of(q4 * 128, 128), 128)] = down * scale
-            mf[rows, pl.ds(pl.multiple_of(512 + q4 * 128, 128), 128)] = side * scale
+            scale = 1.0 / total
+            mf[q4, rows] = down * scale
+            mf[4 + q4, rows] = side * scale
             return 0
 
         lax.fori_loop(0, 4 * count, one, 0)
 
-    forwards = {}
-    forwards[0] = forward(0)
+    forward_0 = forward(0)
     arrive(0)
-    for copy in statics:
-        copy.wait_recv()
-    match_copy = remote(wgot.at[2, 8], wgot.at[2, 0], ms_ss, ms_rs, ynext)
-    wr = jnp.dot(turn, wgot[0, 1:9].reshape(128, 512), preferred_element_type=F32)
-    wup_s[...] = jnp.concatenate([wr[120:128], wr[120:128]], axis=0).astype(BF)
-    up_copy = remote(wup_s, wup_r, wu_ss, wu_rs, below)
-    wc = jnp.dot(turn, wgot[1, 1:9].reshape(128, 512), preferred_element_type=F32)
-    m = jnp.dot(turn, wgot[2, 1:9].reshape(128, 512), preferred_element_type=F32)
-    coef[0] = wr
-    coef[2] = wc
-    coef[7] = m
-
-    forwards[0].wait_recv()
+    forward_0.wait_recv()
     convert(0)
     hs[0] = tmp[0:32].astype(BF)
     halo_up = remote(hs.at[0], hr.at[1], hl_ss.at[0], hl_rs.at[0], above)
-    forwards[1] = forward(1)
+    forward_1 = forward(1)
     arrive(1)
-    match_copy.wait_recv()
-    up_copy.wait_recv()
-    wr = coef[0]
-    wc = coef[2]
-    m = coef[7]
-    mp = jnp.dot(turn, wgot[2, 0:8].reshape(128, 512), preferred_element_type=F32)
-    wu = jnp.concatenate([wup_r[...].astype(F32)[0:8], wr[0:120]], axis=0)
-    wl = jnp.where(col_ids == 0, 0.0, pltpu.roll(wc, 1, 1))
-    diagonal = wr + wu + wc + wl + m + mp
-    step = RELAX_RATE / (1.0 + diagonal)
-    coef[0] = step * wr
-    coef[1] = step * wu
-    coef[2] = step * wc
-    coef[3] = step * wl
-    coef[4] = step * m
-    coef[5] = step * mp
-    coef[6] = 1.0 - step * diagonal
-    coef[8] = step
-
-    forwards[1].wait_recv()
+    forward_1.wait_recv()
     convert(1)
-    forwards[3] = forward(3)
+    forward_3 = forward(3)
     score(1, 6)
     arrive(3)
-    forwards[3].wait_recv()
+    forward_3.wait_recv()
     convert(3)
     hs[1] = tmp[96:128].astype(BF)
     halo_down = remote(hs.at[1], hr.at[0], hl_ss.at[1], hl_rs.at[1], below)
-    forwards[2] = forward(2)
+    forward_2 = forward(2)
     score(13, 2)
-    arrive(2)
-    forwards[2].wait_recv()
-    convert(2)
-    score(7, 6)
     halo_up.wait_recv()
     halo_down.wait_recv()
     tmp[0:32] = jnp.where(g == 0, 0.0, hr[0].astype(F32))
@@ -296,41 +276,78 @@
     lax.fori_loop(0, 3, foot, 0)
     score(0, 1)
     score(15, 1)
-
-    u = iota((32, 128), 0)
-    v = iota((32, 128), 1)
-    pick_f = (v == jnp.where(u < 16, u * 8 + 7, (u - 16) * 8)).astype(F32)
-    pick = pick_f.astype(BF)
-    u = iota((128, 32), 1)
-    v = iota((128, 32), 0)
-    put_f = (v == jnp.where(u < 16, u * 8, (u - 16) * 8 + 7)).astype(F32)
-    put = put_f.astype(BF)
-    e0s[...] = jnp.dot(pick_f[0:16], mf[...], precision=HIGH, preferred_element_type=F32)
+    arrive(2)
+    forward_2.wait_recv()
+    convert(2)
+
+    for copy in statics:
+        copy.wait_recv()
+    match_copy = remote(wgot.at[2, 8], wgot.at[2, 0], ms_ss, ms_rs, ynext)
+    every = slice(0, 128)
+    wr = jnp.dot(turn, wgot[0, 1:9].reshape(128, 512), preferred_element_type=F32)
+    wup_s[...] = jnp.concatenate([wr[120:128], wr[120:128]], axis=0).astype(BF)
+    up_copy = remote(wup_s, wup_r, wu_ss, wu_rs, below)
+    store(coef.at[0], every, wr)
+    store(coef.at[2], every, jnp.dot(turn, wgot[1, 1:9].reshape(128, 512), preferred_element_type=F32))
+    store(coef.at[7], every, jnp.dot(turn, wgot[2, 1:9].reshape(128, 512), preferred_element_type=F32))
+
+    score(7, 6)
+
+    def strided(s, start=0):
+        return pl.ds(start + s, NODES, stride=8)
+
+    for p in range(8):
+        e0s[:, 128 * p : 128 * p + 128] = mf[p, strided(7), :] * coef[7, p % 4, strided(7), :]
     e0 = remote(e0s, e0r, e0_ss, e0_rs, ynext)
+
+    match_copy.wait_recv()
+    up_copy.wait_recv()
+    store(coef.at[5], every, jnp.dot(turn, wgot[2, 0:8].reshape(128, 512), preferred_element_type=F32))
+    sub = iota((8, 512), 0)
+    col = iota((8, 512), 1)
+    for p in range(8):
+        for o in range(2):
+            rel[o, p, 0:8] = jnp.zeros((8, 128), F32)
+            rel[o, p, 136:144] = jnp.zeros((8, 128), F32)
+    wu_next = wup_r[...].astype(F32)[0:8]
+    for i in range(NODES):
+        rows = slice(8 * i, 8 * i + 8)
+        wu = wu_next
+        wr = load(coef.at[0], rows)
+        wu_next = wr
+        wc = load(coef.at[2], rows)
+        m = load(coef.at[7], rows)
+        mp = load(coef.at[5], rows)
+        wl = jnp.where(col == 0, 0.0, pltpu.roll(wc, 1, 1))
+        diagonal = wr + wu + wc + wl + m + mp
+        step = RELAX_RATE / (1.0 + diagonal)
+        for k, factor in enumerate((wr, wu, wc, wl, m, mp)):
+            store(coef.at[k], rows, step * factor)
+        store(coef.at[6], rows, 1.0 - step * diagonal)
+        store(coef.at[7], rows, step)
+        for h in range(2):
+            own = m * load(mf, rows, 4 * h)
+            pushed = step * (jnp.where(sub == 0, 0.0, pltpu.roll(own, 1, 0)) - own)
+            store(mf, rows, pushed, 4 * h)
+    for p in range(8):
+        cn7[p] = coef[4, p % 4, strided(7), :]
+        cp0[p] = coef[5, p % 4, strided(0), :]
     e0.wait_recv()
-    zed[...] = jnp.dot(put_f[:, 0:16], e0r[...], precision=HIGH, preferred_element_type=F32)
-    sub = iota((8, 512), 0)
-
-    def begin(i, _):
-        rows = pl.ds(pl.multiple_of(i * 8, 8), 8)
-        for h in range(2):
-            cols = slice(512 * h, 512 * h + 512)
-            own = mf[rows, cols]
-            before = jnp.where(sub == 0, zed[rows, cols], pltpu.roll(own, 1, 0))
-            pushed = coef[8, rows] * (before - own)
-            mf[rows, cols] = pushed
-            rel[0, pl.ds(pl.multiple_of(i * 8 + 8, 8), 8), cols] = pushed
-        return 0
-
-    lax.fori_loop(0, NODES, begin, 0)
+    for p in range(8):
+        step0 = coef[7, p % 4, strided(0), :]
+        mf[p, strided(0), :] = mf[p, strided(0), :] + step0 * e0r[:, 128 * p : 128 * p + 128]
+    for p in range(8):
+        rel[0, p, 8:136] = mf[p]
 
     def relax(n, _):
         old = n % 2
         new = 1 - old
-        body = rel[old, 8:136]
-        ys[n] = jnp.dot(pick, body.astype(BF), preferred_element_type=F32).astype(BF)
-        rs_[n, 0] = jnp.concatenate([body[0:8, 0:512], body[0:8, 512:1024]], axis=0).astype(BF)
-        rs_[n, 1] = jnp.concatenate([body[120:128, 0:512], body[120:128, 512:1024]], axis=0).astype(BF)
+        for p in range(8):
+            ys[n, 0:16, 128 * p : 128 * p + 128] = rel[old, p, strided(7, 8), :].astype(BF)
+            ys[n, 16:32, 128 * p : 128 * p + 128] = rel[old, p, strided(0, 8), :].astype(BF)
+        for j, rows in enumerate((slice(8, 16), slice(128, 136))):
+            ends = [load(rel.at[old], rows, 4 * h) for h in range(2)]
+            rs_[n, j] = jnp.concatenate(ends, axis=0).astype(BF)
         copies = []
         for j, (src, dst, dev) in enumerate((
             (ys.at[n, pl.ds(0, 16)], yr.at[n, pl.ds(0, 16)], ynext),
@@ -344,41 +361,52 @@
             )
             copy.start()
             copies.append(copy)
-        for copy in copies:
-            copy.wait()
-        zed[...] = jnp.dot(put, yr[n], preferred_element_type=F32)
+
+        def some(i4, _):
+            for i in range(4):
+                start = pl.multiple_of(i4 * 32, 32)
+                rows = pl.ds(pl.multiple_of(start + 8 * i, 8), 8)
+                mid = pl.ds(pl.multiple_of(start + 8 * i + 8, 8), 8)
+                far = pl.ds(pl.multiple_of(start + 8 * i + 16, 8), 8)
+                cs = [load(coef.at[k], rows) for k in range(7)]
+                inner_n = jnp.where(sub == 7, 0.0, cs[4])
+                inner_p = jnp.where(sub == 0, 0.0, cs[5])
+                for h in range(2):
+                    own = load(rel.at[old], mid, 4 * h)
+                    acc = load(mf, rows, 4 * h) + cs[6] * own
+                    acc += cs[0] * load(rel.at[old], far, 4 * h) + cs[1] * load(rel.at[old], rows, 4 * h)
+                    acc += cs[2] * pltpu.roll(own, 511, 1) + cs[3] * pltpu.roll(own, 1, 1)
+                    acc += inner_n * pltpu.roll(own, 7, 0) + inner_p * pltpu.roll(own, 1, 0)
+                    store(rel.at[new], mid, acc, 4 * h)
+            return 0
+
+        lax.fori_loop(0, NODES // 4, some, 0)
+        copies[2].wait()
+        copies[3].wait()
+        high = rr_[n, 1].astype(F32)
         low = rr_[n, 0].astype(F32)
-        high = rr_[n, 1].astype(F32)
-        rel[old, 136:144, 0:512] = low[0:8]
-        rel[old, 136:144, 512:1024] = low[8:16]
-        rel[old, 0:8, 0:512] = high[0:8]
-        rel[old, 0:8, 512:1024] = high[8:16]
-
-        def one(i, _):
-            rows = pl.ds(pl.multiple_of(i * 8, 8), 8)
-            mid = pl.ds(pl.multiple_of(i * 8 + 8, 8), 8)
-            far = pl.ds(pl.multiple_of(i * 8 + 16, 8), 8)
-            cs = [coef[k, rows] for k in range(7)]
-            for h in range(2):
-                cols = slice(512 * h, 512 * h + 512)
-                own = rel[old, mid, cols]
-                edge = zed[rows, cols]
-                acc = mf[rows, cols] + cs[6] * own
-                acc += cs[0] * rel[old, far, cols] + cs[1] * rel[old, rows, cols]
-                acc += cs[2] * pltpu.roll(own, 511, 1) + cs[3] * pltpu.roll(own, 1, 1)
-                acc += cs[4] * jnp.where(sub == 7, edge, pltpu.roll(own, 7, 0))
-                acc += cs[5] * jnp.where(sub == 0, edge, pltpu.roll(own, 1, 0))
-                rel[new, mid, cols] = acc
-            return 0
-
-        lax.fori_loop(0, NODES, one, 0)
+        for p in range(8):
+            part = slice(8 * (p // 4), 8 * (p // 4) + 8)
+            cols = slice(128 * (p % 4), 128 * (p % 4) + 128)
+            rel[new, p, 128:136] = rel[new, p, 128:136] + coef[0, p % 4, 120:128] * low[part, cols]
+            rel[new, p, 8:16] = rel[new, p, 8:16] + coef[1, p % 4, 0:8] * high[part, cols]
+        copies[0].wait()
+        copies[1].wait()
+        for p in range(8):
+            cols = slice(128 * p, 128 * p + 128)
+            edge = rel[new, p, strided(0, 8), :] + cp0[p] * yr[n, 0:16, cols].astype(F32)
+            rel[new, p, strided(0, 8), :] = edge
+            edge = rel[new, p, strided(7, 8), :] + cn7[p] * yr[n, 16:32, cols].astype(F32)
+            rel[new, p, strided(7, 8), :] = edge
         return 0
 
     lax.fori_loop(0, ITERS - 1, relax, 0)
 
-    final = jnp.dot(back, rel[(ITERS - 1) % 2, 8:136], precision=HIGH, preferred_element_type=F32)
-    ret[0] = final[:, 0:512]
-    ret[1] = final[:, 512:1024]
+    done = (ITERS - 1) % 2
+    for s in range(8):
+        for p in range(8):
+            cols = slice(128 * (p % 4), 128 * (p % 4) + 128)
+            ret[p // 4, 16 * s : 16 * s + 16, cols] = rel[done, p, strided(s, 8), :]
     place = pl.ds(pl.multiple_of(16 * c, 16), 16)
     returns = []
     for k in range(1, 8):
@@ -407,9 +435,13 @@
     return pl.pallas_call(
         kernel,
         out_shape=jax.ShapeDtypeStruct((2, 1, 128, 512), F32),
-        in_specs=[pl.BlockSpec(memory_space=pltpu.SMEM), whole, whole, whole],
+        in_specs=[pl.BlockSpec(memory_space=pltpu.HBM)] * 4,
         out_specs=whole,
         scratch_shapes=[
+            pltpu.SMEM((NOFF, 2), jnp.int32),
+            vm((512, 2048), BF),
+            vm((2, 128, 512), jnp.int32),
+            vm((128, 512), jnp.int32),
             vm((512, 2048), BF),
             vm((9, PIX, 2048), BF),
             vm((3, 128, 512), BF),
@@ -421,12 +453,13 @@
             vm((128, 2048), F32),
             vm((2, 32, 2048), BF),
             vm((2, 32, 2048), BF),
-            vm((9, 128, 512), F32),
-            vm((128, 1024), F32),
+            vm((8, 4, 128, 128), F32),
+            vm((8, 16, 128), F32),
+            vm((8, 16, 128), F32),
+            vm((8, 128, 128), F32),
             vm((16, 1024), F32),
             vm((16, 1024), F32),
-            vm((2, 144, 1024), F32),
-            vm((128, 1024), F32),
+            vm((2, 8, 144, 128), F32),
             vm((ITERS - 1, 32, 1024), BF),
             vm((ITERS - 1, 32, 1024), BF),
             vm((ITERS - 1, 2, 16, 512), BF),
@@ -434,7 +467,7 @@
             vm((2, 128, 512), F32),
             dma((4, 8)), dma((4, 8)), dma((4,)), dma((4,)), dma((8,)), dma((8,)), dma, dma,
             dma((2,)), dma((2,)), dma, dma, dma, dma,
-            dma((ITERS - 1, 4)), dma((ITERS - 1, 4)), dma((8,)), dma((8,)),
+            dma((ITERS - 1, 4)), dma((ITERS - 1, 4)), dma((8,)), dma((8,)), dma((8,)),
         ],
         compiler_params=pltpu.CompilerParams(
             collective_id=0, has_side_effects=True, vmem_limit_bytes=48 * 1024 * 1024

time: 121 us -> 89.5 us (0.74)
  Pallas kernels: 115 us -> 83.7 us
    pallas_call x1, Pallas kernels: 115 us -> 83.7 us  [shards(): pl.pallas_call(kernel, out_shape=jax.ShapeDtypeStruct((2, 1, 128, 512), F...]
where the time goes in v2:
time: 89.5 us; the launch traced here: 88.9 us
  Pallas kernels  83.7 us (94%)
  local copies, waits for them, and re-layouts  5.15 us (6%)
    pallas_call x1, Pallas kernels, shards(): pl.pallas_call(kernel, out_shape=jax.ShapeDtypeStruct((2, 1, 128, 512), F...  83.7 us
    unnamed x8, local copies, waits for them, and re-layouts  5.15 us

profile of v2, /device:TPU:0, one launch (start us, length us, event | category | flops | bytes accessed | tf_op | source)
XLA Modules:
  0.0 88.9 jit_solution(2784696002906891944)
XLA Ops:
  0.0 0.8 copy.5.off_hbm
  0.8 0.0 copy-start
  0.8 1.6 %copy-done = bf16[1,512,2048]{2,1,0:T(8,128)(2,1)S(1)} copy-done((bf16[1,512,2048]{2,1,0:T(8,128)(2,1)S(1)}, bf16[1,512,2048]{2,1,0:T(8,128)(2,1)}, u32[]{:S(2)}) %copy-start) | copy-done | bytes 2097176
  2.4 0.0 copy-start.1
  2.4 1.0 %copy-done.1 = s32[2,1,128,512]{3,2,1,0:T(8,128)S(1)} copy-done((s32[2,1,128,512]{3,2,1,0:T(8,128)S(1)}, s32[2,1,128,512]{3,2,1,0:T(8,128)}, u32[]{:S(2)}) %copy-start.1) | copy-done | bytes 524312
  3.4 0.0 copy-start.2
  3.4 0.9 %copy-done.2 = s32[1,128,512]{2,1,0:T(8,128)S(1)} copy-done((s32[1,128,512]{2,1,0:T(8,128)S(1)}, s32[1,128,512]{2,1,0:T(8,128)}, u32[]{:S(2)}) %copy-start.2) | copy-done | bytes 262168
  4.4 83.7 %shard_map.46 = f32[2,1,128,512]{3,2,1,0:T(8,128)S(1)} custom-call(s32[25,2]{1,0:T(8,128)S(1)} %copy.5.off_hbm, bf16[1,512,2048]{2,1,0:T(8,128)(2,1)S(1)} %copy-done, s32[2,1,128,512]{3,2,1,0:T(8,128)S(1)} %copy-done.1, s32[1,128,512]{2,1,0:T(8,128)S(1)} %copy-done.2), custom_call_target="tpu_custom_call" | custom-call | tf_op jit(solution)/shard_map/pallas_call | solution.py:435
  88.1 0.8 copy.7
Async XLA Ops:
  0.8 1.6 %copy-start = (bf16[1,512,2048]{2,1,0:T(8,128)(2,1)S(1)}, bf16[1,512,2048]{2,1,0:T(8,128)(2,1)}, u32[]{:S(2)}) copy-start(bf16[1,512,2048]{2,1,0:T(8,128)(2,1)} %x_hbm.1) | copy-start | bytes 6291460
  2.4 1.0 %copy-start.1 = (s32[2,1,128,512]{3,2,1,0:T(8,128)S(1)}, s32[2,1,128,512]{3,2,1,0:T(8,128)}, u32[]{:S(2)}) copy-start(s32[2,1,128,512]{3,2,1,0:T(8,128)} %sp_hbm.1) | copy-start | bytes 1572868
  3.4 0.9 %copy-start.2 = (s32[1,128,512]{2,1,0:T(8,128)S(1)}, s32[1,128,512]{2,1,0:T(8,128)}, u32[]{:S(2)}) copy-start(s32[1,128,512]{2,1,0:T(8,128)} %va_hbm.1) | copy-start | bytes 786436

commit v3 on v2

--- a/solution.py
+++ b/solution.py
@@ -46,7 +46,7 @@
 
 
 def kernel(
-    off_hbm, x_hbm, sp_hbm, va_hbm, out_ref,
+    off_hbm, x_hbm, sp_hbm, va_hbm, early_ref, late_ref,
     off_ref, x_ref, sp_ref, va_ref, xs, got, ws, wgot, wup_s, wup_r, cur, nxt, tmp, hs, hr, coef, cn7, cp0, mf, e0s, e0r, rel, ys, yr, rs_, rr_, ret,
     img_ss, img_rs, fwd_ss, fwd_rs, st_ss, st_rs, ms_ss, ms_rs, hl_ss, hl_rs, wu_ss, wu_rs, e0_ss, e0_rs,
     it_ss, it_rs, rt_ss, rt_rs, in_sem,
@@ -153,8 +153,6 @@
             copy.start()
             started.append(copy)
     statics = [static_copy(k) for k in range(1, 8)]
-    for copy in statics:
-        copy.start()
     got[e] = xs[pl.ds(pl.multiple_of(64 * c, 64), 64)]
     wgot[:, e + 1] = ws[:, pl.ds(pl.multiple_of(16 * c, 16), 16)]
 
@@ -193,12 +191,15 @@
                 carry = left[q + 1, w] if q < 3 else jnp.zeros((8, 128), F32)
                 nxt[base + 10 * q + w + 7] = jnp.where(lane == 127, carry, left[q, w])
 
-    def convert(blk):
+    def convert_own(blk):
         rows = slice(16 * blk, 16 * blk + 16)
         here = jnp.dot(turn, got[0:8, rows].reshape(128, 2048), preferred_element_type=F32)
         for r in range(16):
             for p in range(16):
                 cur[(16 * blk + r) * 16 + p] = here[8 * r : 8 * r + 8, 128 * p : 128 * p + 128]
+
+    def convert(blk):
+        rows = slice(16 * blk, 16 * blk + 16)
         tmp[...] = jnp.dot(turn, got[1:9, rows].reshape(128, 2048), preferred_element_type=F32)
 
         def one(r, _):
@@ -214,7 +215,7 @@
             mine = [[cur[((4 * row + q) * 4 + q4) * 4 + w] for w in range(4)] for q in range(4)]
             scores = []
             for k in range(NOFF):
-                at = (4 * row + off_ref[k, 0] + RAD) * SPAN + 10 * q4 + off_ref[k, 1] + RAD
+                at = (4 * row + off_ref[0, k] + RAD) * SPAN + 10 * q4 + off_ref[1, k] + RAD
                 parts = []
                 for q in range(4):
                     p = [mine[q][w] * nxt[at + (q * SPAN + w)] for w in range(4)]
@@ -229,8 +230,8 @@
             for k in range(NOFF):
                 soft = jnp.exp(SHARPNESS * (scores[k] - top))
                 total += soft
-                down += soft * off_ref[k, 0].astype(F32)
-                side += soft * off_ref[k, 1].astype(F32)
+                down += soft * off_ref[0, k].astype(F32)
+                side += soft * off_ref[1, k].astype(F32)
             rows = pl.ds(pl.multiple_of(row * 8, 8), 8)
             scale = 1.0 / total
             mf[q4, rows] = down * scale
@@ -239,66 +240,61 @@
 
         lax.fori_loop(0, 4 * count, one, 0)
 
+    def halves(rows):
+        return jnp.concatenate([tmp[rows, 0:1024], tmp[rows, 1024:2048]], axis=0).astype(BF)
+
+    def halo(j, row, outside):
+        came = jnp.where(outside, 0.0, hr[j].astype(F32))
+        tmp[0:24, 0:1024] = came[0:24]
+        tmp[0:24, 1024:2048] = came[24:48]
+
+        def one(r, _):
+            expand(row + r, pl.multiple_of(r * 8, 8))
+            return 0
+
+        lax.fori_loop(0, 3, one, 0)
+
+    every = slice(0, 128)
     forward_0 = forward(0)
     arrive(0)
+    convert_own(0)
     forward_0.wait_recv()
     convert(0)
-    hs[0] = tmp[0:32].astype(BF)
-    halo_up = remote(hs.at[0], hr.at[1], hl_ss.at[0], hl_rs.at[0], above)
+    hs[0] = halves(slice(0, 24))
     forward_1 = forward(1)
     arrive(1)
+    convert_own(1)
     forward_1.wait_recv()
     convert(1)
     forward_3 = forward(3)
-    score(1, 6)
+    score(1, 4)
     arrive(3)
+    convert_own(3)
     forward_3.wait_recv()
     convert(3)
-    hs[1] = tmp[96:128].astype(BF)
+    hs[1] = halves(slice(104, 128))
+    forward_2 = forward(2)
+    for copy in statics:
+        copy.start()
+    halo_up = remote(hs.at[0], hr.at[1], hl_ss.at[0], hl_rs.at[0], above)
     halo_down = remote(hs.at[1], hr.at[0], hl_ss.at[1], hl_rs.at[1], below)
-    forward_2 = forward(2)
+    score(5, 2)
+    arrive(2)
+    convert_own(2)
     score(13, 2)
-    halo_up.wait_recv()
-    halo_down.wait_recv()
-    tmp[0:32] = jnp.where(g == 0, 0.0, hr[0].astype(F32))
-    tmp[32:64] = jnp.where(g == 31, 0.0, hr[1].astype(F32))
-
-    def head(r, _):
-        expand(r - 3, pl.multiple_of(r * 8 + 8, 8))
-        return 0
-
-    lax.fori_loop(0, 3, head, 0)
-
-    def foot(r, _):
-        expand(PIX + r, pl.multiple_of(r * 8 + 32, 8))
-        return 0
-
-    lax.fori_loop(0, 3, foot, 0)
-    score(0, 1)
-    score(15, 1)
-    arrive(2)
     forward_2.wait_recv()
     convert(2)
 
     for copy in statics:
         copy.wait_recv()
     match_copy = remote(wgot.at[2, 8], wgot.at[2, 0], ms_ss, ms_rs, ynext)
-    every = slice(0, 128)
     wr = jnp.dot(turn, wgot[0, 1:9].reshape(128, 512), preferred_element_type=F32)
     wup_s[...] = jnp.concatenate([wr[120:128], wr[120:128]], axis=0).astype(BF)
     up_copy = remote(wup_s, wup_r, wu_ss, wu_rs, below)
     store(coef.at[0], every, wr)
     store(coef.at[2], every, jnp.dot(turn, wgot[1, 1:9].reshape(128, 512), preferred_element_type=F32))
-    store(coef.at[7], every, jnp.dot(turn, wgot[2, 1:9].reshape(128, 512), preferred_element_type=F32))
-
+    store(coef.at[8], every, jnp.dot(turn, wgot[2, 1:9].reshape(128, 512), preferred_element_type=F32))
     score(7, 6)
-
-    def strided(s, start=0):
-        return pl.ds(start + s, NODES, stride=8)
-
-    for p in range(8):
-        e0s[:, 128 * p : 128 * p + 128] = mf[p, strided(7), :] * coef[7, p % 4, strided(7), :]
-    e0 = remote(e0s, e0r, e0_ss, e0_rs, ynext)
 
     match_copy.wait_recv()
     up_copy.wait_recv()
@@ -316,7 +312,7 @@
         wr = load(coef.at[0], rows)
         wu_next = wr
         wc = load(coef.at[2], rows)
-        m = load(coef.at[7], rows)
+        m = load(coef.at[8], rows)
         mp = load(coef.at[5], rows)
         wl = jnp.where(col == 0, 0.0, pltpu.roll(wc, 1, 1))
         diagonal = wr + wu + wc + wl + m + mp
@@ -325,21 +321,59 @@
             store(coef.at[k], rows, step * factor)
         store(coef.at[6], rows, 1.0 - step * diagonal)
         store(coef.at[7], rows, step)
+
+    def strided(s, start=0):
+        return pl.ds(start + s, NODES, stride=8)
+
+    for p in range(8):
+        cn7[p] = coef[4, p % 4, strided(7), :]
+        cp0[p] = coef[5, p % 4, strided(0), :]
+
+    halo_up.wait_recv()
+    halo(1, PIX, g == 31)
+    halo_down.wait_recv()
+    halo(0, -RAD, g == 0)
+    score(0, 1)
+    score(15, 1)
+
+    for p in range(8):
+        e0s[:, 128 * p : 128 * p + 128] = mf[p, strided(7), :] * coef[8, p % 4, strided(7), :]
+    e0 = remote(e0s, e0r, e0_ss, e0_rs, ynext)
+    for i in range(NODES):
+        rows = slice(8 * i, 8 * i + 8)
+        m = load(coef.at[8], rows)
+        step = load(coef.at[7], rows)
         for h in range(2):
             own = m * load(mf, rows, 4 * h)
             pushed = step * (jnp.where(sub == 0, 0.0, pltpu.roll(own, 1, 0)) - own)
             store(mf, rows, pushed, 4 * h)
-    for p in range(8):
-        cn7[p] = coef[4, p % 4, strided(7), :]
-        cp0[p] = coef[5, p % 4, strided(0), :]
+            store(rel.at[0], slice(8 * i + 8, 8 * i + 16), pushed, 4 * h)
     e0.wait_recv()
     for p in range(8):
         step0 = coef[7, p % 4, strided(0), :]
-        mf[p, strided(0), :] = mf[p, strided(0), :] + step0 * e0r[:, 128 * p : 128 * p + 128]
-    for p in range(8):
-        rel[0, p, 8:136] = mf[p]
-
-    def relax(n, _):
+        first = mf[p, strided(0), :] + step0 * e0r[:, 128 * p : 128 * p + 128]
+        mf[p, strided(0), :] = first
+        rel[0, p, strided(0, 8), :] = first
+
+    def send_back(src, dst, half):
+        for k in range(1, 8):
+            other = (e + k) % 8
+            copy = pltpu.make_async_remote_copy(
+                src_ref=src.at[:, pl.ds(pl.multiple_of(16 * other, 16), 16)], dst_ref=dst.at[:, 0, place],
+                send_sem=rt_ss.at[half, k], recv_sem=rt_rs.at[half, k], device_id=peers[k - 1], device_id_type=MESH,
+            )
+            copy.start()
+            returns.append(copy)
+        own = pltpu.make_async_copy(
+            src.at[:, pl.ds(pl.multiple_of(16 * e, 16), 16)], dst.at[:, 0, place], rt_ss.at[half, 0]
+        )
+        own.start()
+        owns.append(own)
+
+    returns, owns = [], []
+    place = pl.ds(pl.multiple_of(16 * c, 16), 16)
+
+    def relax(n, last):
         old = n % 2
         new = 1 - old
         for p in range(8):
@@ -361,6 +395,13 @@
             )
             copy.start()
             copies.append(copy)
+        if last:
+            for s in range(8):
+                for p in range(8):
+                    cols = slice(128 * (p % 4), 128 * (p % 4) + 128)
+                    part = rel[old, p, strided(s, 8), :].astype(BF)
+                    ret[0, p // 4, 16 * s : 16 * s + 16, cols] = part
+            send_back(ret.at[0], early_ref, 0)
 
         def some(i4, _):
             for i in range(4):
@@ -398,32 +439,31 @@
             rel[new, p, strided(0, 8), :] = edge
             edge = rel[new, p, strided(7, 8), :] + cn7[p] * yr[n, 16:32, cols].astype(F32)
             rel[new, p, strided(7, 8), :] = edge
+
+    def several(n, _):
+        relax(n, False)
         return 0
 
-    lax.fori_loop(0, ITERS - 1, relax, 0)
+    lax.fori_loop(0, ITERS - 2, several, 0)
+    relax(ITERS - 2, True)
 
     done = (ITERS - 1) % 2
     for s in range(8):
         for p in range(8):
             cols = slice(128 * (p % 4), 128 * (p % 4) + 128)
-            ret[p // 4, 16 * s : 16 * s + 16, cols] = rel[done, p, strided(s, 8), :]
-    place = pl.ds(pl.multiple_of(16 * c, 16), 16)
-    returns = []
-    for k in range(1, 8):
-        other = (e + k) % 8
-        copy = pltpu.make_async_remote_copy(
-            src_ref=ret.at[:, pl.ds(pl.multiple_of(16 * other, 16), 16)], dst_ref=out_ref.at[:, 0, place],
-            send_sem=rt_ss.at[k], recv_sem=rt_rs.at[k], device_id=peers[k - 1], device_id_type=MESH,
-        )
-        copy.start()
-        returns.append(copy)
-    out_ref[:, 0, place] = ret[:, pl.ds(pl.multiple_of(16 * e, 16), 16)]
-    for k in range(1, 8):
-        oc = part_of((e + 8 - k) % 8, t)
-        pltpu.make_async_remote_copy(
-            src_ref=ret.at[:, pl.ds(0, 16)], dst_ref=out_ref.at[:, 0, pl.ds(pl.multiple_of(16 * oc, 16), 16)],
-            send_sem=rt_ss.at[k], recv_sem=rt_rs.at[k], device_id=peers[k - 1], device_id_type=MESH,
-        ).wait_recv()
+            rows = slice(16 * s, 16 * s + 16)
+            sent = ret[0, p // 4, rows, cols].astype(F32)
+            ret[1, p // 4, rows, cols] = (rel[done, p, strided(s, 8), :] - sent).astype(BF)
+    send_back(ret.at[1], late_ref, 1)
+    for half, dst in enumerate((early_ref, late_ref)):
+        for k in range(1, 8):
+            oc = part_of((e + 8 - k) % 8, t)
+            pltpu.make_async_remote_copy(
+                src_ref=ret.at[half, :, pl.ds(0, 16)], dst_ref=dst.at[:, 0, pl.ds(pl.multiple_of(16 * oc, 16), 16)],
+                send_sem=rt_ss.at[half, k], recv_sem=rt_rs.at[half, k], device_id=peers[k - 1], device_id_type=MESH,
+            ).wait_recv()
+    for copy in owns:
+        copy.wait()
     for copy in returns + started + statics + sends:
         copy.wait_send()
 
@@ -431,14 +471,13 @@
 def shards(images, offsets, springs, validity):
     dma = pltpu.SemaphoreType.DMA
     vm = pltpu.VMEM
-    whole = pl.BlockSpec(memory_space=pltpu.VMEM)
-    return pl.pallas_call(
+    early, late = pl.pallas_call(
         kernel,
-        out_shape=jax.ShapeDtypeStruct((2, 1, 128, 512), F32),
+        out_shape=[jax.ShapeDtypeStruct((2, 1, 128, 512), BF)] * 2,
         in_specs=[pl.BlockSpec(memory_space=pltpu.HBM)] * 4,
-        out_specs=whole,
+        out_specs=[pl.BlockSpec(memory_space=pltpu.HBM)] * 2,
         scratch_shapes=[
-            pltpu.SMEM((NOFF, 2), jnp.int32),
+            pltpu.SMEM((2, NOFF), jnp.int32),
             vm((512, 2048), BF),
             vm((2, 128, 512), jnp.int32),
             vm((128, 512), jnp.int32),
@@ -451,9 +490,9 @@
             vm((PIX * 16, 8, 128), F32),
             vm(((PIX + 2 * RAD) * SPAN, 8, 128), F32),
             vm((128, 2048), F32),
-            vm((2, 32, 2048), BF),
-            vm((2, 32, 2048), BF),
-            vm((8, 4, 128, 128), F32),
+            vm((2, 48, 1024), BF),
+            vm((2, 48, 1024), BF),
+            vm((9, 4, 128, 128), F32),
             vm((8, 16, 128), F32),
             vm((8, 16, 128), F32),
             vm((8, 128, 128), F32),
@@ -464,15 +503,16 @@
             vm((ITERS - 1, 32, 1024), BF),
             vm((ITERS - 1, 2, 16, 512), BF),
             vm((ITERS - 1, 2, 16, 512), BF),
-            vm((2, 128, 512), F32),
+            vm((2, 2, 128, 512), BF),
             dma((4, 8)), dma((4, 8)), dma((4,)), dma((4,)), dma((8,)), dma((8,)), dma, dma,
             dma((2,)), dma((2,)), dma, dma, dma, dma,
-            dma((ITERS - 1, 4)), dma((ITERS - 1, 4)), dma((8,)), dma((8,)), dma((8,)),
+            dma((ITERS - 1, 4)), dma((ITERS - 1, 4)), dma((2, 8)), dma((2, 8)), dma((8,)),
         ],
         compiler_params=pltpu.CompilerParams(
-            collective_id=0, has_side_effects=True, vmem_limit_bytes=48 * 1024 * 1024
+            collective_id=0, has_side_effects=True, vmem_limit_bytes=61 * 1024 * 1024
         ),
-    )(offsets, images, springs, validity)
+    )(offsets.T, images, springs, validity)
+    return early.astype(F32) + late.astype(F32)
 
 
 def solution(mesh):

time: 89.5 us -> 83.2 us (0.930)
  local copies, waits for them, and re-layouts: 5.15 us -> 0 us
  Pallas kernels: 83.7 us -> 81.1 us
  other arithmetic: 0 us -> 1.9 us
    unnamed x8 -> x0, local copies, waits for them, and re-layouts: 5.15 us -> none
    pallas_call x1, Pallas kernels: 83.7 us -> 81.1 us  [shards(): pl.pallas_call(kernel, out_shape=[jax.ShapeDtypeStruct((2, 1, 128, 512),...]
    add x0 -> x1, other arithmetic: none -> 1.9 us  [shards(): return early.astype(F32) + late.astype(F32)]
where the time goes in v3:
time: 83.2 us; the launch traced here: 83 us
  Pallas kernels  81.1 us (97%)
  other arithmetic  1.9 us (2%)
    pallas_call x1, Pallas kernels, shards(): pl.pallas_call(kernel, out_shape=[jax.ShapeDtypeStruct((2, 1, 128, 512),...  81.1 us
    add x1, other arithmetic, shards(): return early.astype(F32) + late.astype(F32)  1.9 us

profile of v3, /device:TPU:0, one launch (start us, length us, event | category | flops | bytes accessed | tf_op | source)
XLA Modules:
  0.0 83.0 jit_solution(4866285859570141501)
XLA Ops:
  0.0 81.1 %shard_map.46 = (bf16[2,1,128,512]{3,2,1,0:T(8,128)(2,1)}, bf16[2,1,128,512]{3,2,1,0:T(8,128)(2,1)}) custom-call(s32[2,25]{1,0:T(2,128)} %bitcast.1, bf16[1,512,2048]{2,1,0:T(8,128)(2,1)} %x_hbm.1, s32[2,1,128,512]{3,2,1,0:T(8,128)} %sp_hbm.1, s32[1,128,512]{2,1,0:T(8,128)} %va_hbm.1), custom_call_target="tpu_custom_call" | custom-call | tf_op jit(solution)/shard_map/pallas_call | solution.py:474
  81.1 1.9 %convert_add_fusion = f32[2,1,128,512]{3,2,1,0:T(8,128)} fusion(bf16[2,1,128,512]{3,2,1,0:T(8,128)(2,1)} %get-tuple-element.8, bf16[2,1,128,512]{3,2,1,0:T(8,128)(2,1)} %get-tuple-element.7), kind=kLoop, calls=%fused_computation | loop fusion | flops 393216 | bytes 1048576 | tf_op jit(solution)/shard_map/add | solution.py:515

commit v4 on v3

--- a/solution.py
+++ b/solution.py
@@ -10,6 +10,7 @@
 SHARPNESS = 0.5
 RELAX_RATE = 0.8
 NOFF = 25
+LOG2_E = 1.4426950408889634
 
 BF = jnp.bfloat16
 F32 = jnp.float32
@@ -47,9 +48,9 @@
 
 def kernel(
     off_hbm, x_hbm, sp_hbm, va_hbm, early_ref, late_ref,
-    off_ref, x_ref, sp_ref, va_ref, xs, got, ws, wgot, wup_s, wup_r, cur, nxt, tmp, hs, hr, coef, cn7, cp0, mf, e0s, e0r, rel, ys, yr, rs_, rr_, ret,
+    off_ref, x_ref, sp_ref, va_ref, xs, got, ws, wgot, wup_s, wup_r, cur, nxt, tmp, hs, hr, coef, cn7, cp0, mf, e0s, e0r, corner, step_s, step_n, step_e, delta, rel, ys, yr, rs_, rr_, ret,
     img_ss, img_rs, fwd_ss, fwd_rs, st_ss, st_rs, ms_ss, ms_rs, hl_ss, hl_rs, wu_ss, wu_rs, e0_ss, e0_rs,
-    it_ss, it_rs, rt_ss, rt_rs, in_sem,
+    co_ss, co_rs, sp_ss, sp_rs, it_ss, it_rs, rt_ss, rt_rs, in_sem,
 ):
     sec = lax.axis_index("sec")
     t = lax.axis_index("strip")
@@ -57,19 +58,21 @@
     c = part_of(e, t)
     g = t * 8 + c
 
-    def row_device(h):
+    def row_device(h, group):
         h = (h + 32) % 32
         tt = h // 8
-        return (8 * y + member_of(h % 8, tt), tt)
+        return (8 * group + member_of(h % 8, tt), tt)
 
     peers = [(8 * y + (e + k) % 8, t) for k in range(1, 8)]
     ynext = ((sec + 8) % 32, t)
     yprev = ((sec + 24) % 32, t)
-    below = row_device(g + 1)
-    above = row_device(g - 1)
+    below = row_device(g + 1, y)
+    above = row_device(g - 1, y)
+    later, former = (y + 1) % 4, (y + 3) % 4
     barrier = pltpu.get_barrier_semaphore()
     everyone = peers + [ynext, yprev, below, above]
-    for d in everyone:
+    senders = [row_device(g + 1, former), row_device(g - 1, former)]
+    for d in everyone + senders:
         pl.semaphore_signal(barrier, inc=1, device_id=d, device_id_type=MESH)
 
     chunks = []
@@ -104,14 +107,14 @@
     wc_own = jnp.where(col_ids == 511, 0.0, 0.25 * sp_ref[1].astype(F32))
     m_own = jnp.where(sec == lax.axis_size("sec") - 1, 0.0, va_ref[...].astype(F32))
     ws[0] = wr_own.astype(BF)
-    ws[1] = wc_own.astype(BF)
-    ws[2] = m_own.astype(BF)
+    ws[1] = m_own.astype(BF)
+    ws[2] = wc_own.astype(BF)
 
     a = iota((128, 128), 0)
     b = iota((128, 128), 1)
     turn = (b == (a % 8) * 16 + a // 8).astype(F32).astype(BF)
 
-    pl.semaphore_wait(barrier, len(everyone))
+    pl.semaphore_wait(barrier, len(everyone) + len(senders))
 
     sends = []
 
@@ -138,12 +141,13 @@
             recv_sem=img_rs.at[blk, s], device_id=peers[0], device_id_type=MESH,
         )
 
-    def static_copy(k):
+    def static_copy(k, part):
+        own = pl.ds(0, 2) if part == 0 else pl.ds(2, 1)
         other = (e + k) % 8
         oc = part_of(other, t)
         return pltpu.make_async_remote_copy(
-            src_ref=ws.at[:, pl.ds(pl.multiple_of(16 * oc, 16), 16)], dst_ref=wgot.at[:, e + 1],
-            send_sem=st_ss.at[k], recv_sem=st_rs.at[k], device_id=peers[k - 1], device_id_type=MESH,
+            src_ref=ws.at[own, pl.ds(pl.multiple_of(16 * oc, 16), 16)], dst_ref=wgot.at[own, e + 1],
+            send_sem=st_ss.at[part, k], recv_sem=st_rs.at[part, k], device_id=peers[k - 1], device_id_type=MESH,
         )
 
     started = []
@@ -152,7 +156,9 @@
             copy = image_copy(blk, k)
             copy.start()
             started.append(copy)
-    statics = [static_copy(k) for k in range(1, 8)]
+    statics_a = [static_copy(k, 0) for k in range(1, 8)]
+    statics_b = [static_copy(k, 1) for k in range(1, 8)]
+    statics = statics_a + statics_b
     got[e] = xs[pl.ds(pl.multiple_of(64 * c, 64), 64)]
     wgot[:, e + 1] = ws[:, pl.ds(pl.multiple_of(16 * c, 16), 16)]
 
@@ -228,7 +234,7 @@
             down = jnp.zeros((8, 128), F32)
             side = jnp.zeros((8, 128), F32)
             for k in range(NOFF):
-                soft = jnp.exp(SHARPNESS * (scores[k] - top))
+                soft = jnp.exp2((SHARPNESS * LOG2_E) * (scores[k] - top))
                 total += soft
                 down += soft * off_ref[0, k].astype(F32)
                 side += soft * off_ref[1, k].astype(F32)
@@ -238,7 +244,7 @@
             mf[4 + q4, rows] = side * scale
             return 0
 
-        lax.fori_loop(0, 4 * count, one, 0)
+        lax.fori_loop(0, 4 * count, one, 0, unroll=2)
 
     def halves(rows):
         return jnp.concatenate([tmp[rows, 0:1024], tmp[rows, 1024:2048]], axis=0).astype(BF)
@@ -270,35 +276,37 @@
     score(1, 4)
     arrive(3)
     convert_own(3)
+    for copy in statics:
+        copy.start()
     forward_3.wait_recv()
     convert(3)
     hs[1] = halves(slice(104, 128))
     forward_2 = forward(2)
-    for copy in statics:
-        copy.start()
     halo_up = remote(hs.at[0], hr.at[1], hl_ss.at[0], hl_rs.at[0], above)
     halo_down = remote(hs.at[1], hr.at[0], hl_ss.at[1], hl_rs.at[1], below)
     score(5, 2)
     arrive(2)
     convert_own(2)
     score(13, 2)
-    forward_2.wait_recv()
-    convert(2)
-
-    for copy in statics:
+
+    for copy in statics_a:
         copy.wait_recv()
-    match_copy = remote(wgot.at[2, 8], wgot.at[2, 0], ms_ss, ms_rs, ynext)
+    match_copy = remote(wgot.at[1, 8], wgot.at[1, 0], ms_ss, ms_rs, ynext)
     wr = jnp.dot(turn, wgot[0, 1:9].reshape(128, 512), preferred_element_type=F32)
     wup_s[...] = jnp.concatenate([wr[120:128], wr[120:128]], axis=0).astype(BF)
     up_copy = remote(wup_s, wup_r, wu_ss, wu_rs, below)
     store(coef.at[0], every, wr)
-    store(coef.at[2], every, jnp.dot(turn, wgot[1, 1:9].reshape(128, 512), preferred_element_type=F32))
-    store(coef.at[8], every, jnp.dot(turn, wgot[2, 1:9].reshape(128, 512), preferred_element_type=F32))
+    store(coef.at[8], every, jnp.dot(turn, wgot[1, 1:9].reshape(128, 512), preferred_element_type=F32))
+    forward_2.wait_recv()
+    convert(2)
     score(7, 6)
+    for copy in statics_b:
+        copy.wait_recv()
+    store(coef.at[2], every, jnp.dot(turn, wgot[2, 1:9].reshape(128, 512), preferred_element_type=F32))
 
     match_copy.wait_recv()
     up_copy.wait_recv()
-    store(coef.at[5], every, jnp.dot(turn, wgot[2, 0:8].reshape(128, 512), preferred_element_type=F32))
+    store(coef.at[5], every, jnp.dot(turn, wgot[1, 0:8].reshape(128, 512), preferred_element_type=F32))
     sub = iota((8, 512), 0)
     col = iota((8, 512), 1)
     for p in range(8):
@@ -328,6 +336,14 @@
     for p in range(8):
         cn7[p] = coef[4, p % 4, strided(7), :]
         cp0[p] = coef[5, p % 4, strided(0), :]
+        delta[p] = jnp.zeros((32, 128), F32)
+    for p in range(4):
+        step_s[p] = coef[7, p, strided(0), :]
+    steps = [
+        remote(step_s, step_n, sp_ss.at[0], sp_rs.at[0], yprev),
+        remote(coef.at[7, :, pl.ds(0, 8)], step_e.at[1], sp_ss.at[1], sp_rs.at[1], above),
+        remote(coef.at[7, :, pl.ds(120, 8)], step_e.at[0], sp_ss.at[2], sp_rs.at[2], below),
+    ]
 
     halo_up.wait_recv()
     halo(1, PIX, g == 31)
@@ -339,6 +355,10 @@
     for p in range(8):
         e0s[:, 128 * p : 128 * p + 128] = mf[p, strided(7), :] * coef[8, p % 4, strided(7), :]
     e0 = remote(e0s, e0r, e0_ss, e0_rs, ynext)
+    corners = [
+        remote(e0s.at[pl.ds(8, 8)], corner.at[0], co_ss.at[0], co_rs.at[0], row_device(g + 1, later)),
+        remote(e0s.at[pl.ds(0, 8)], corner.at[1], co_ss.at[1], co_rs.at[1], row_device(g - 1, later)),
+    ]
     for i in range(NODES):
         rows = slice(8 * i, 8 * i + 8)
         m = load(coef.at[8], rows)
@@ -348,12 +368,27 @@
             pushed = step * (jnp.where(sub == 0, 0.0, pltpu.roll(own, 1, 0)) - own)
             store(mf, rows, pushed, 4 * h)
             store(rel.at[0], slice(8 * i + 8, 8 * i + 16), pushed, 4 * h)
-    e0.wait_recv()
-    for p in range(8):
-        step0 = coef[7, p % 4, strided(0), :]
-        first = mf[p, strided(0), :] + step0 * e0r[:, 128 * p : 128 * p + 128]
-        mf[p, strided(0), :] = first
-        rel[0, p, strided(0, 8), :] = first
+
+    def missing(new):
+        e0.wait_recv()
+        for p in range(8):
+            delta[p, 8:24] = coef[7, p % 4, strided(0), :] * e0r[:, 128 * p : 128 * p + 128]
+        for h in range(2):
+            own = load(delta, slice(8, 24), 4 * h)
+
+            def factor(k, s):
+                return jnp.concatenate([coef[k, q, strided(s), :] for q in range(4)], axis=1)
+
+            acc = own + factor(6, 0) * own
+            acc += factor(0, 0) * load(delta, slice(9, 25), 4 * h) + factor(1, 0) * load(delta, slice(7, 23), 4 * h)
+            acc += factor(2, 0) * pltpu.roll(own, 511, 1) + factor(3, 0) * pltpu.roll(own, 1, 1)
+            aside = factor(5, 1) * own
+            for q in range(4):
+                p = 4 * h + q
+                cols = slice(128 * q, 128 * q + 128)
+                rel[new, p, strided(0, 8), :] = rel[new, p, strided(0, 8), :] + acc[:, cols]
+                rel[new, p, strided(1, 8), :] = rel[new, p, strided(1, 8), :] + aside[:, cols]
+                mf[p, strided(0), :] = mf[p, strided(0), :] + own[:, cols]
 
     def send_back(src, dst, half):
         for k in range(1, 8):
@@ -373,7 +408,7 @@
     returns, owns = [], []
     place = pl.ds(pl.multiple_of(16 * c, 16), 16)
 
-    def relax(n, last):
+    def relax(n, first, last):
         old = n % 2
         new = 1 - old
         for p in range(8):
@@ -422,6 +457,10 @@
             return 0
 
         lax.fori_loop(0, NODES // 4, some, 0)
+        if first:
+            missing(new)
+            for copy in corners + steps:
+                copy.wait_recv()
         copies[2].wait()
         copies[3].wait()
         high = rr_[n, 1].astype(F32)
@@ -429,23 +468,32 @@
         for p in range(8):
             part = slice(8 * (p // 4), 8 * (p // 4) + 8)
             cols = slice(128 * (p % 4), 128 * (p % 4) + 128)
-            rel[new, p, 128:136] = rel[new, p, 128:136] + coef[0, p % 4, 120:128] * low[part, cols]
-            rel[new, p, 8:16] = rel[new, p, 8:16] + coef[1, p % 4, 0:8] * high[part, cols]
+            over, under = high[part, cols], low[part, cols]
+            if first:
+                at = slice(128 * p, 128 * p + 128)
+                over += jnp.where(sub[:, 0:128] == 0, step_e[0, p % 4] * corner[0, 7:8, at], 0.0)
+                under += jnp.where(sub[:, 0:128] == 0, step_e[1, p % 4] * corner[1, 0:1, at], 0.0)
+            rel[new, p, 128:136] = rel[new, p, 128:136] + coef[0, p % 4, 120:128] * under
+            rel[new, p, 8:16] = rel[new, p, 8:16] + coef[1, p % 4, 0:8] * over
         copies[0].wait()
         copies[1].wait()
         for p in range(8):
             cols = slice(128 * p, 128 * p + 128)
             edge = rel[new, p, strided(0, 8), :] + cp0[p] * yr[n, 0:16, cols].astype(F32)
             rel[new, p, strided(0, 8), :] = edge
-            edge = rel[new, p, strided(7, 8), :] + cn7[p] * yr[n, 16:32, cols].astype(F32)
+            after = yr[n, 16:32, cols].astype(F32)
+            if first:
+                after += step_n[p % 4] * e0s[:, cols]
+            edge = rel[new, p, strided(7, 8), :] + cn7[p] * after
             rel[new, p, strided(7, 8), :] = edge
 
     def several(n, _):
-        relax(n, False)
+        relax(n, False, False)
         return 0
 
-    lax.fori_loop(0, ITERS - 2, several, 0)
-    relax(ITERS - 2, True)
+    relax(0, True, False)
+    lax.fori_loop(1, ITERS - 2, several, 0)
+    relax(ITERS - 2, False, True)
 
     done = (ITERS - 1) % 2
     for s in range(8):
@@ -498,14 +546,20 @@
             vm((8, 128, 128), F32),
             vm((16, 1024), F32),
             vm((16, 1024), F32),
+            vm((2, 8, 1024), F32),
+            vm((4, 16, 128), F32),
+            vm((4, 16, 128), F32),
+            vm((2, 4, 8, 128), F32),
+            vm((8, 32, 128), F32),
             vm((2, 8, 144, 128), F32),
             vm((ITERS - 1, 32, 1024), BF),
             vm((ITERS - 1, 32, 1024), BF),
             vm((ITERS - 1, 2, 16, 512), BF),
             vm((ITERS - 1, 2, 16, 512), BF),
             vm((2, 2, 128, 512), BF),
-            dma((4, 8)), dma((4, 8)), dma((4,)), dma((4,)), dma((8,)), dma((8,)), dma, dma,
+            dma((4, 8)), dma((4, 8)), dma((4,)), dma((4,)), dma((2, 8)), dma((2, 8)), dma, dma,
             dma((2,)), dma((2,)), dma, dma, dma, dma,
+            dma((2,)), dma((2,)), dma((3,)), dma((3,)),
             dma((ITERS - 1, 4)), dma((ITERS - 1, 4)), dma((2, 8)), dma((2, 8)), dma((8,)),
         ],
         compiler_params=pltpu.CompilerParams(

time: 83.2 us -> 80.8 us (0.971)
  Pallas kernels: 81.1 us -> 78.7 us
    pallas_call x1, Pallas kernels: 81.1 us -> 78.7 us  [shards(): pl.pallas_call(kernel, out_shape=[jax.ShapeDtypeStruct((2, 1, 128, 512),...]
where the time goes in v4:
time: 80.8 us; the launch traced here: 80.6 us
  Pallas kernels  78.7 us (97%)
  other arithmetic  1.9 us (2%)
    pallas_call x1, Pallas kernels, shards(): pl.pallas_call(kernel, out_shape=[jax.ShapeDtypeStruct((2, 1, 128, 512),...  78.7 us
    add x1, other arithmetic, shards(): return early.astype(F32) + late.astype(F32)  1.9 us

profile of v4, /device:TPU:0, one launch (start us, length us, event | category | flops | bytes accessed | tf_op | source)
XLA Modules:
  0.0 80.6 jit_solution(2788098787134350924)
XLA Ops:
  0.0 78.7 %shard_map.46 = (bf16[2,1,128,512]{3,2,1,0:T(8,128)(2,1)}, bf16[2,1,128,512]{3,2,1,0:T(8,128)(2,1)}) custom-call(s32[2,25]{1,0:T(2,128)} %bitcast.1, bf16[1,512,2048]{2,1,0:T(8,128)(2,1)} %x_hbm.1, s32[2,1,128,512]{3,2,1,0:T(8,128)} %sp_hbm.1, s32[1,128,512]{2,1,0:T(8,128)} %va_hbm.1), custom_call_target="tpu_custom_call" | custom-call | tf_op jit(solution)/shard_map/pallas_call | solution.py:522
  78.7 1.9 %convert_add_fusion = f32[2,1,128,512]{3,2,1,0:T(8,128)} fusion(bf16[2,1,128,512]{3,2,1,0:T(8,128)(2,1)} %get-tuple-element.8, bf16[2,1,128,512]{3,2,1,0:T(8,128)(2,1)} %get-tuple-element.7), kind=kLoop, calls=%fused_computation | loop fusion | flops 393216 | bytes 1048576 | tf_op jit(solution)/shard_map/add | solution.py:569
